TPU v7x, 128 devices: a whole 4x4x4 slice. The times are simulated.
128 devices in a mesh: sector: 16 (over y_hi, x, core), axial: 8 (over z, y_lo).
Axes of the slice: x: 4, y: 4 (y_hi: 2, y_lo: 2; y = y_hi * 2 + y_lo), z: 4, core: 2. Of those that a mesh axis runs over, the one named last changes fastest.
Arguments:
- flow_state: float32 [5, 256, 256, 128], P(None, 'sector', 'axial'), may hold values from -6 to 6
- damping: float32 [256, 256, 128], P('sector', 'axial'), may hold values from 0.05 to 0.5
- jacobians: float32 [3, 5, 5], replicated, may hold values from -2.5 to 2.5
- face_weight: float32 [5, 256, 256], P(None, 'sector', 'axial'), may hold values from -3 to 3
- phase_shift: int32 [4], replicated, may hold values from 0 to 255, as said below
- face_list: int32 [128, 128, 4], P(('sector', 'axial')), may hold values from 0 to 3, as said below
- face_count: int32 [128, 128], P(('sector', 'axial')), may hold values from 0 to 4, as said below
- arrival_bin: int32 [128, 128, 4, 2, 128], P(('sector', 'axial')), may hold values from 0 to 123
- arrival_fraction: float32 [128, 128, 4, 2, 128], P(('sector', 'axial')), may hold values from 0 to 1
- arrival_gain: float32 [128, 128, 4, 2, 128], P(('sector', 'axial')), may hold values from 0.005 to 0.05
Outputs:
- new_state: float32 [5, 256, 256, 128], P(None, 'sector', 'axial')
- signal: float32 [256, 128], P(('sector', 'axial'))
Inputs may be any that keep to these rules, and one draw needn't show every extreme that they name: `phase_shift`: in one substep the offset lies between 128 and 143, in another it is 255, and in another 0. `face_list`: the entries of one list are distinct face blocks of the source device; entries at or past the count are padding. `face_count`: some observer owner has 4 live entries from every source device.
All inputs are finite; a program needn't handle non-finite values.
Results may differ from a plain program's by a relative error of at most 0.0003.
Values sent between devices are 32-bit elements; how exact they have to be, the bound alone decides.
A program may use at most 128 MiB of HBM per device.

v0:
```python
import jax
import jax.numpy as jnp
from jax import lax
from jax.sharding import PartitionSpec as P

FACE = 128
NBIN = 128


time_step = 0.3
viscosity = 0.05


def with_halo(cells, sides, width, closed):
    for axis, dim in sides:
        count = lax.axis_size(axis)
        ends = count if closed else count - 1
        head = lax.slice_in_dim(cells, 0, width, axis=dim)
        tail = lax.slice_in_dim(cells, cells.shape[dim] - width, cells.shape[dim], axis=dim)
        cells = jnp.concatenate(
            [
                lax.ppermute(tail, axis, [(i, (i + 1) % count) for i in range(ends)]),
                cells,
                lax.ppermute(head, axis, [((i + 1) % count, i) for i in range(ends)]),
            ],
            axis=dim,
        )
    return cells


def apply_jacobian(matrix, flow_field):
    return jnp.einsum("ij,jtzr->itzr", matrix, flow_field, precision=lax.Precision.HIGHEST)


def roll_gathered(interface_row, offset):
    row_width = interface_row.shape[1]
    gathered = lax.all_gather(interface_row, "sector", axis=1, tiled=True)
    cycle_cells = gathered.shape[1]
    first_cell = lax.axis_index("sector") * row_width
    doubled = jnp.concatenate([gathered, gathered], axis=1)
    slice_start = jnp.mod(first_cell - offset, cycle_cells)
    return lax.dynamic_slice_in_dim(doubled, slice_start, row_width, 1)


def tendency(flow_field, jacobians, damping, rotation):
    theta_pad = with_halo(flow_field, (("sector", 1),), 1, True)
    axial_pad = with_halo(flow_field, (("axial", 2),), 1, False)
    position = lax.axis_index("axial")
    middle = lax.axis_size("axial") // 2
    is_aft = position == middle
    is_front = position == middle - 1
    lower_ghost = axial_pad[:, :, 0]
    upper_ghost = axial_pad[:, :, -1]
    interface_row = jnp.where(is_aft, lower_ghost, upper_ghost)
    cycle_cells = flow_field.shape[1] * lax.axis_size("sector")
    offset = jnp.mod(jnp.where(is_aft, rotation, -rotation), cycle_cells)
    rolled = roll_gathered(interface_row, offset)
    lower_ghost = jnp.where(is_aft, rolled, lower_ghost)
    upper_ghost = jnp.where(is_front, rolled, upper_ghost)
    theta_plus = theta_pad[:, 2:]
    theta_minus = theta_pad[:, :-2]
    axial_plus = jnp.concatenate([axial_pad[:, :, 2:-1], upper_ghost[:, :, None]], axis=2)
    axial_minus = jnp.concatenate([lower_ghost[:, :, None], axial_pad[:, :, 1:-2]], axis=2)
    zero_column = jnp.zeros_like(flow_field[..., :1])
    radial_plus = jnp.concatenate([flow_field[..., 1:], zero_column], axis=3)
    radial_minus = jnp.concatenate([zero_column, flow_field[..., :-1]], axis=3)
    advection = (
        apply_jacobian(jacobians[0], 0.5 * (theta_plus - theta_minus))
        + apply_jacobian(jacobians[1], 0.5 * (axial_plus - axial_minus))
        + apply_jacobian(jacobians[2], 0.5 * (radial_plus - radial_minus))
    )
    laplacian = (
        theta_plus
        + theta_minus
        + axial_plus
        + axial_minus
        + radial_plus
        + radial_minus
        - 6.0 * flow_field
    )
    return viscosity * laplacian - advection - damping[None] * flow_field


def outgoing(flow_field, face_weight, block_lists, counts):
    surface = flow_field[:, :, :, flow_field.shape[3] // 2]
    values = jnp.sum(face_weight * surface, axis=0)
    blocks = values.shape[0] * values.shape[1] // FACE
    values = values.reshape(blocks, FACE)
    selector = block_lists[:, :, None] == jnp.arange(blocks, dtype=jnp.int32)[None, None, :]
    live_slot = jnp.arange(block_lists.shape[1], dtype=jnp.int32)[None, :] < counts[:, None]
    selector = (selector & live_slot[:, :, None]).astype(jnp.float32)
    return jnp.einsum("dcb,bf->dcf", selector, values, precision=lax.Precision.HIGHEST)


def shifted(column, offset):
    if offset == 0:
        return column
    return jnp.concatenate([jnp.zeros((offset,), jnp.float32), column[:-offset]])


def accumulate(received, bins, fractions, gains):
    samples = received.shape[2]

    def one_observer(inputs):
        bin_plane, fraction_plane, gain_plane = inputs
        amplitude = gain_plane[:, :, None, :] * received
        lower_part = amplitude * (1.0 - fraction_plane)[:, :, None, :]
        upper_part = amplitude * fraction_plane[:, :, None, :]
        weights = jnp.concatenate([lower_part, upper_part], axis=2)
        weights = jnp.swapaxes(weights, 2, 3).reshape(-1, 2 * samples)
        selector = (
            bin_plane.reshape(-1)[:, None] == jnp.arange(NBIN, dtype=jnp.int32)[None, :]
        ).astype(jnp.float32)
        binned = jnp.einsum("mb,mw->wb", selector, weights, precision=lax.Precision.HIGHEST)
        result = jnp.zeros((NBIN,), jnp.float32)
        for sample in range(samples):
            result = (
                result
                + shifted(binned[sample], sample)
                + shifted(binned[samples + sample], sample + 1)
            )
        return result

    return lax.map(
        one_observer,
        (jnp.moveaxis(bins, 2, 0), jnp.moveaxis(fractions, 2, 0), jnp.moveaxis(gains, 2, 0)),
    )


def local(
    flow_state,
    damping,
    jacobians,
    face_weight,
    phase_shift,
    face_list,
    face_count,
    arrival_bin,
    arrival_fraction,
    arrival_gain,
):
    block_lists = face_list[0]
    counts = face_count[0]
    pieces = []

    def record(flow_field):
        parcel = outgoing(flow_field, face_weight, block_lists, counts)
        parcel = lax.all_to_all(
            parcel, ("sector", "axial"), split_axis=0, concat_axis=0, tiled=True
        )
        pieces.append(parcel)

    record(flow_state)
    rate_one = tendency(flow_state, jacobians, damping, phase_shift[0])
    section_two = flow_state + 0.5 * time_step * rate_one
    record(section_two)
    rate_two = tendency(section_two, jacobians, damping, phase_shift[1])
    section_three = flow_state + 0.5 * time_step * rate_two
    record(section_three)
    rate_three = tendency(section_three, jacobians, damping, phase_shift[2])
    section_four = flow_state + time_step * rate_three
    record(section_four)
    rate_four = tendency(section_four, jacobians, damping, phase_shift[3])
    new_state = flow_state + time_step / 6.0 * (
        rate_one + 2.0 * rate_two + 2.0 * rate_three + rate_four
    )
    stacked = jnp.stack(pieces, axis=2)
    signal = accumulate(stacked, arrival_bin[0], arrival_fraction[0], arrival_gain[0])
    return (new_state, signal)


def solution(mesh):
    return jax.shard_map(
        local,
        mesh=mesh,
        in_specs=(
            P(None, "sector", "axial", None),
            P("sector", "axial", None),
            P(),
            P(None, "sector", "axial"),
            P(),
            P(("sector", "axial"), None, None),
            P(("sector", "axial"), None),
            P(("sector", "axial"), None, None, None, None),
            P(("sector", "axial"), None, None, None, None),
            P(("sector", "axial"), None, None, None, None),
        ),
        out_specs=(P(None, "sector", "axial", None), P(("sector", "axial"), None)),
        check_vma=False,
    )
```

profile of v0, /device:TPU:1, one launch (start us, length us, event | category | flops | bytes accessed | tf_op | source)
XLA Modules:
  0.0 348.8 jit_solution(13835663701181472042)
XLA Ops:
  3.5 4.6 %collective-permute-start.2 = (f32[5,16,1,128]{3,1,0,2:T(8,128)}, f32[5,16,1,128]{3,1,0,2:T(8,128)}, u32[]{:S(2)}, u32[]{:S(2)}) collective-permute-start(f32[5,16,1,128]{3,1,0,2:T(8,128)} %get-tuple-element.135), channel_id=1, source_target_pairs={{0,1},{1,2},{2,3},{3,4},{4,5},{5,6},{6,7},{8,9},{9,10},{10,11},{11... | collective-permute-start | bytes 122888 | tf_op jit(solution)/shard_map/ppermute | solution.py:22
  18.3 3.6 %fusion.22 = f32[16,32,128,5]{2,3,1,0:T(8,128)} fusion(f32[5,16,32,128]{3,1,0,2:T(8,128)S(1)} %subtract_multiply_fusion.9, f32[1,5,5]{2,0,1:T(1,128)S(1)} %get-tuple-element.141), kind=kOutput, calls=%fused_computation.40 | convolution fusion | flops 19660800 | bytes 2621540 | tf_op jit(solution)/shard_map/ij,jtzr->itzr/dot_general | solution.py:32
  36.2 25.6 %all_gather.12 = f32[5,256,128]{2,1,0:T(8,128)S(1)} all-gather(f32[5,16,128]{2,1,0:T(8,128)S(1)} %bitcast_select_fusion.10), channel_id=1, replica_groups=mesh['sector'=16,'axial'=8] {'sector'}, dimensions={1}, use_global_device_ids=true | all-gather | bytes 696320 | tf_op jit(solution)/shard_map/all_gather | solution.py:37
  68.6 2.6 fusion.26
  71.3 6.3 %multiply_add_fusion.1 = (f32[5,16,32,128]{3,1,0,2:T(8,128)S(1)}, f32[5,16,32,128]{3,1,0,2:T(8,128)}) fusion(f32[5,16,32,128]{3,2,1,0:T(8,128)S(1)} %copy-done, f32[5,16,32,128]{3,2,1,0:T(8,128)S(1)} %copy-done.21, f32[16,32,128,5]{2,3,1,0:T(8,128)S(1)} %copy-done.17, f32[16,32,128,5]{2,3,1,0:T(8,128)S(1)} %fusion.24, f32[16,32,128,5]{2,3,1,0:T(8,128)S(1)} %fusion.26, ...), kind=kLoop, calls=%fused_computation.100 | loop fusion | flops 5898240 | bytes 15872000 | tf_op jit(solution)/shard_map/add | solution.py:155
  81.3 4.0 %collective-permute-start.6 = (f32[5,16,1,128]{3,1,0,2:T(8,128)}, f32[5,16,1,128]{3,1,0,2:T(8,128)}, u32[]{:S(2)}, u32[]{:S(2)}) collective-permute-start(f32[5,16,1,128]{3,1,0,2:T(8,128)} %get-tuple-element.125), channel_id=1, source_target_pairs={{0,1},{1,2},{2,3},{3,4},{4,5},{5,6},{6,7},{8,9},{9,10},{10,11},{11... | collective-permute-start | bytes 122888 | tf_op jit(solution)/shard_map/ppermute | solution.py:22
  87.4 3.6 %fusion.16 = f32[16,32,128,5]{2,3,1,0:T(8,128)} fusion(f32[5,16,32,128]{3,1,0,2:T(8,128)S(1)} %subtract_multiply_fusion.6, f32[1,5,5]{2,0,1:T(1,128)S(1)} %get-tuple-element.141), kind=kOutput, calls=%fused_computation.34 | convolution fusion | flops 19660800 | bytes 2621540 | tf_op jit(solution)/shard_map/ij,jtzr->itzr/dot_general | solution.py:32
  97.6 21.7 %all_gather.13 = f32[5,256,128]{2,1,0:T(8,128)S(1)} all-gather(f32[5,16,128]{2,1,0:T(8,128)S(1)} %bitcast_select_fusion.7), channel_id=1, replica_groups=mesh['sector'=16,'axial'=8] {'sector'}, dimensions={1}, use_global_device_ids=true | all-gather | bytes 696320 | tf_op jit(solution)/shard_map/all_gather | solution.py:37
  129.6 4.4 %broadcast_multiply_fusion = (f32[5,16,32,128]{3,1,0,2:T(8,128)S(1)}, f32[5,16,32,128]{3,1,0,2:T(8,128)}) fusion(f32[5,16,32,128]{3,1,0,2:T(8,128)S(1)} %get-tuple-element.93, f32[16,32,128]{2,0,1:T(8,128)S(1)} %copy-done.26, f32[16,32,128,5]{2,3,1,0:T(8,128)S(1)} %copy-done.18, f32[16,32,128,5]{2,1,3,0:T(8,128)S(1)} %copy_add_fusion.6, ...), kind=kLoop, calls=%fused_computation.112 | loop fusion | flops 5570560 | bytes 12201984 | tf_op jit(solution)/shard_map/mul | solution.py:158
  135.4 4.4 %collective-permute-start.10 = (f32[5,16,1,128]{3,1,0,2:T(8,128)S(1)}, f32[5,16,1,128]{3,1,0,2:T(8,128)S(1)}, u32[]{:S(2)}, u32[]{:S(2)}) collective-permute-start(f32[5,16,1,128]{3,1,0,2:T(8,128)S(1)} %bitcast.205), channel_id=1, source_target_pairs={{0,1},{1,2},{2,3},{3,4},{4,5},{5,6},{6,7},{8,9},{9,10},{10,11},{11... | collective-permute-start | bytes 122888 | tf_op jit(solution)/shard_map/ppermute | solution.py:22
  141.8 2.6 fusion.10
  147.0 22.0 %all_gather.14 = f32[5,256,128]{2,1,0:T(8,128)S(1)} all-gather(f32[5,16,128]{2,1,0:T(8,128)S(1)} %bitcast_select_fusion.4), channel_id=1, replica_groups=mesh['sector'=16,'axial'=8] {'sector'}, dimensions={1}, use_global_device_ids=true | all-gather | bytes 696320 | tf_op jit(solution)/shard_map/all_gather | solution.py:37
  169.4 2.6 fusion.12
  172.3 2.6 fusion.14
  174.9 3.1 multiply_add_fusion
  184.9 8.4 %all-to-all-start = ((f32[128,4,128]{2,1,0:T(4,128)}), f32[128,4,128]{2,1,0:T(4,128)}, u32[]{:S(2)}, u32[]{:S(2)}) async-start(f32[128,4,128]{2,1,0:T(4,128)} %copy.296), calls=%async_computation | async-start | bytes 524288 | tf_op jit(solution)/shard_map/all_to_all | solution.py:148
  199.3 3.3 collective-permute-start.14
  206.1 3.9 %fusion.4 = f32[16,32,128,5]{2,3,1,0:T(8,128)} fusion(f32[5,16,32,128]{3,2,1,0:T(8,128)S(1)} %subtract_multiply_fusion, f32[1,5,5]{2,0,1:T(1,128)S(1)} %get-tuple-element.141), kind=kOutput, calls=%fused_computation.22 | convolution fusion | flops 19660800 | bytes 2621540 | tf_op jit(solution)/shard_map/ij,jtzr->itzr/dot_general | solution.py:32
  210.0 3.3 fusion.36
  213.6 25.5 %all_gather.15 = f32[5,256,128]{2,1,0:T(8,128)S(1)} all-gather(f32[5,16,128]{2,1,0:T(8,128)S(1)} %bitcast_select_fusion.1), channel_id=1, replica_groups=mesh['sector'=16,'axial'=8] {'sector'}, dimensions={1}, use_global_device_ids=true | all-gather | bytes 696320 | tf_op jit(solution)/shard_map/all_gather | solution.py:37
  240.5 7.4 %all-to-all-start.1 = ((f32[128,4,128]{2,1,0:T(4,128)}), f32[128,4,128]{2,1,0:T(4,128)}, u32[]{:S(2)}, u32[]{:S(2)}) async-start(f32[128,4,128]{2,1,0:T(4,128)} %copy.298), calls=%async_computation.1 | async-start | bytes 524288 | tf_op jit(solution)/shard_map/all_to_all | solution.py:148
  248.0 5.2 %fusion.6 = f32[16,32,128,5]{2,3,1,0:T(8,128)} fusion(f32[5,16,32,128]{3,2,1,0:T(8,128)} %subtract_multiply_fusion.1, f32[1,5,5]{2,0,1:T(1,128)S(1)} %get-tuple-element.140), kind=kOutput, calls=%fused_computation.24 | convolution fusion | flops 19660800 | bytes 2621540 | tf_op jit(solution)/shard_map/ij,jtzr->itzr/dot_general | solution.py:32
  255.4 2.9 all-to-all-done.1
  258.2 7.8 %all-to-all-start.2 = ((f32[128,4,128]{2,1,0:T(4,128)}), f32[128,4,128]{2,1,0:T(4,128)}, u32[]{:S(2)}, u32[]{:S(2)}) async-start(f32[128,4,128]{2,1,0:T(4,128)} %copy.299), calls=%async_computation.2 | async-start | bytes 524288 | tf_op jit(solution)/shard_map/all_to_all | solution.py:148
  266.0 5.2 %fusion.8 = f32[16,32,128,5]{2,3,1,0:T(8,128)} fusion(f32[5,16,32,128]{3,2,1,0:T(8,128)} %subtract_multiply_fusion.2, f32[1,5,5]{2,0,1:T(1,128)S(1)} %get-tuple-element.139), kind=kOutput, calls=%fused_computation.26 | convolution fusion | flops 19660800 | bytes 2621540 | tf_op jit(solution)/shard_map/ij,jtzr->itzr/dot_general | solution.py:32
  271.3 4.9 %all-to-all-done.2 = f32[128,4,128]{2,1,0:T(4,128)} async-done(((f32[128,4,128]{2,1,0:T(4,128)}), f32[128,4,128]{2,1,0:T(4,128)}, u32[]{:S(2)}, u32[]{:S(2)}) %all-to-all-start.2) | async-done | bytes 262176 | tf_op jit(solution)/shard_map/all_to_all | solution.py:148
  276.1 5.6 %all-to-all-start.3 = ((f32[128,4,128]{2,1,0:T(4,128)}), f32[128,4,128]{2,1,0:T(4,128)}, u32[]{:S(2)}, u32[]{:S(2)}) async-start(f32[128,4,128]{2,1,0:T(4,128)} %copy.300), calls=%async_computation.3 | async-start | bytes 524288 | tf_op jit(solution)/shard_map/all_to_all | solution.py:148
  281.8 7.3 %fusion.31 = f32[5,16,32,128]{3,2,1,0:T(8,128)} fusion(f32[5,16,32,128]{3,2,1,0:T(8,128)S(1)} %copy-done, f32[5,16,32,128]{3,1,0,2:T(8,128)} %get-tuple-element.146, f32[16,32,128,5]{2,3,1,0:T(8,128)} %fusion.4, f32[16,32,128,5]{2,3,1,0:T(8,128)} %fusion.6, f32[16,32,128,5]{2,3,1,0:T(8,128)} %fusion.8, f32[5,16,32,128]{3,1,0,2:T(8,128)} %get-tuple-element.147, ...), kind=kLoop, calls=%fused_computation.68 | loop fusion | flops 6225920 | bytes 16134144 | tf_op jit(solution)/shard_map/add | solution.py:164
  289.1 3.1 all-to-all-done.3
  294.8 53.0 %while.10 = (s32[]{:T(128)}, f32[2,128]{1,0:T(2,128)S(1)}, f32[2,128,4,128]{3,2,1,0:T(4,128)S(1)}, f32[128,4,4,128]{3,2,1,0:T(4,128)S(1)}, f32[2,128,4,128]{3,2,...) while((s32[]{:T(128)}, f32[2,128]{1,0:T(2,128)S(1)}, ...), condition=%wide.region_5.6_spmd, body=%wide.region_4.5_spmd.sunk | while | flops 815072384 | bytes 12337585 | solution.py:124
  296.0 25.2 %fusion.91 = f32[8,128]{1,0:T(8,128)S(1)} fusion(f32[65536,8]{0,1:T(8,128)S(1)} %bitcast.193, s32[65536]{0:T(1024)S(1)} %bitcast.194), kind=kOutput, calls=%fused_computation.1.clone.2 | convolution fusion | flops 813694976 | bytes 2363392 | tf_op jit(solution)/shard_map/while/body/eval_jaxpr/mb,mw->wb/dot_general | solution.py:114
  322.5 25.2 %fusion.91 = f32[8,128]{1,0:T(8,128)S(1)} fusion(f32[65536,8]{0,1:T(8,128)S(1)} %bitcast.193, s32[65536]{0:T(1024)S(1)} %bitcast.194), kind=kOutput, calls=%fused_computation.1.clone.2 | convolution fusion | flops 813694976 | bytes 2363392 | tf_op jit(solution)/shard_map/while/body/eval_jaxpr/mb,mw->wb/dot_general | solution.py:114
  (213 shorter events, 83.6 us)
Async XLA Ops:
  0.6 8.8 %copy-start = (f32[5,16,32,128]{3,2,1,0:T(8,128)S(1)}, f32[5,16,32,128]{3,2,1,0:T(8,128)}, u32[]{:S(2)}) copy-start(f32[5,16,32,128]{3,2,1,0:T(8,128)} %param.12) | copy-start | bytes 3932164
  2.8 63.6 %copy-start.1 = (f32[5,16,32,128]{3,1,0,2:T(8,128)}, f32[5,16,32,128]{3,1,0,2:T(8,128)S(1)}, u32[]{:S(2)}) copy-start(f32[5,16,32,128]{3,1,0,2:T(8,128)S(1)} %copy.230) | copy-start | bytes 3932164
  3.5 31.8 %collective-permute-start.2 = (f32[5,16,1,128]{3,1,0,2:T(8,128)}, f32[5,16,1,128]{3,1,0,2:T(8,128)}, u32[]{:S(2)}, u32[]{:S(2)}) collective-permute-start(f32[5,16,1,128]{3,1,0,2:T(8,128)} %get-tuple-element.135), channel_id=1, source_target_pairs={{0,1},{1,2},{2,3},{3,4},{4,5},{5,6},{6,7},{8,9},{9,10},{10,11},{11... | collective-permute-start | bytes 122888 | tf_op jit(solution)/shard_map/ppermute | solution.py:22
  8.1 27.1 %collective-permute-start.3 = (f32[5,16,1,128]{3,1,0,2:T(8,128)}, f32[5,16,1,128]{3,1,0,2:T(8,128)S(1)}, u32[]{:S(2)}, u32[]{:S(2)}) collective-permute-start(f32[5,16,1,128]{3,1,0,2:T(8,128)} %get-tuple-element.136), channel_id=1, source_target_pairs={{1,0},{2,1},{3,2},{4,3},{5,4},{6,5},{7,6},{9,8},{10,9},{11,10},{12... | collective-permute-start | bytes 122888 | tf_op jit(solution)/shard_map/ppermute | solution.py:24
  10.2 56.2 %collective-permute-start = (f32[5,1,32,128]{3,1,0,2:T(1,128)}, f32[5,1,32,128]{3,1,0,2:T(1,128)S(1)}, u32[]{:S(2)}, u32[]{:S(2)}) collective-permute-start(f32[5,1,32,128]{3,1,0,2:T(1,128)} %copy.229), channel_id=1, source_target_pairs={{8,0},{16,8},{24,16},{32,24},{40,32},{48,40},{56,48},{64,56},{72,6... | collective-permute-start | bytes 245768 | tf_op jit(solution)/shard_map/ppermute | solution.py:24
  11.9 54.5 %collective-permute-start.1 = (f32[5,1,32,128]{3,1,0,2:T(1,128)}, f32[5,1,32,128]{3,1,0,2:T(1,128)}, u32[]{:S(2)}, u32[]{:S(2)}) collective-permute-start(f32[5,1,32,128]{3,1,0,2:T(1,128)} %copy.231), channel_id=1, source_target_pairs={{0,8},{8,16},{16,24},{24,32},{32,40},{40,48},{48,56},{56,64},{64,7... | collective-permute-start | bytes 245768 | tf_op jit(solution)/shard_map/ppermute | solution.py:22
  35.3 27.3 %copy-start.13 = (f32[5,16,31,128]{3,1,0,2:T(8,128)S(1)}, f32[5,16,31,128]{3,1,0,2:T(8,128)}, u32[]{:S(2)}) copy-start(f32[5,16,31,128]{3,1,0,2:T(8,128)} %get-tuple-element.133) | copy-start | bytes 3809284
  66.4 4.8 %copy-start.21 = (f32[5,16,32,128]{3,2,1,0:T(8,128)S(1)}, f32[5,16,32,128]{3,2,1,0:T(8,128)}, u32[]{:S(2)}) copy-start(f32[5,16,32,128]{3,2,1,0:T(8,128)} %broadcast_multiply_fusion.1) | copy-start | bytes 3932164
  79.5 8.0 %copy-start.7 = (f32[5,16,32,127]{3,1,0,2:T(8,128)}, f32[5,16,32,127]{3,1,0,2:T(8,128)S(1)}, u32[]{:S(2)}) copy-start(f32[5,16,32,127]{3,1,0,2:T(8,128)S(1)} %get-tuple-element.127) | copy-start | bytes 3901444
  79.5 8.0 %copy-start.9 = (f32[5,16,32,127]{3,1,0,2:T(8,128)}, f32[5,16,32,127]{3,1,0,2:T(8,128)S(1)}, u32[]{:S(2)}) copy-start(f32[5,16,32,127]{3,1,0,2:T(8,128)S(1)} %get-tuple-element.128) | copy-start | bytes 3901444
  79.5 44.4 %collective-permute-start.4 = (f32[5,1,32,128]{3,1,0,2:T(1,128)}, f32[5,1,32,128]{3,1,0,2:T(1,128)S(1)}, u32[]{:S(2)}, u32[]{:S(2)}) collective-permute-start(f32[5,1,32,128]{3,1,0,2:T(1,128)} %get-tuple-element.122), channel_id=1, source_target_pairs={{8,0},{16,8},{24,16},{32,24},{40,32},{48,40},{56,48},{64,56},{72,6... | collective-permute-start | bytes 245768 | tf_op jit(solution)/shard_map/ppermute | solution.py:24
  79.9 43.9 %collective-permute-start.5 = (f32[5,1,32,128]{3,1,0,2:T(1,128)}, f32[5,1,32,128]{3,1,0,2:T(1,128)}, u32[]{:S(2)}, u32[]{:S(2)}) collective-permute-start(f32[5,1,32,128]{3,1,0,2:T(1,128)} %get-tuple-element.121), channel_id=1, source_target_pairs={{0,8},{8,16},{16,24},{24,32},{32,40},{40,48},{48,56},{56,64},{64,7... | collective-permute-start | bytes 245768 | tf_op jit(solution)/shard_map/ppermute | solution.py:22
  81.3 15.4 %collective-permute-start.6 = (f32[5,16,1,128]{3,1,0,2:T(8,128)}, f32[5,16,1,128]{3,1,0,2:T(8,128)}, u32[]{:S(2)}, u32[]{:S(2)}) collective-permute-start(f32[5,16,1,128]{3,1,0,2:T(8,128)} %get-tuple-element.125), channel_id=1, source_target_pairs={{0,1},{1,2},{2,3},{3,4},{4,5},{5,6},{6,7},{8,9},{9,10},{10,11},{11... | collective-permute-start | bytes 122888 | tf_op jit(solution)/shard_map/ppermute | solution.py:22
  85.3 11.4 %collective-permute-start.7 = (f32[5,16,1,128]{3,1,0,2:T(8,128)}, f32[5,16,1,128]{3,1,0,2:T(8,128)S(1)}, u32[]{:S(2)}, u32[]{:S(2)}) collective-permute-start(f32[5,16,1,128]{3,1,0,2:T(8,128)} %get-tuple-element.126), channel_id=1, source_target_pairs={{1,0},{2,1},{3,2},{4,3},{5,4},{6,5},{7,6},{9,8},{10,9},{11,10},{12... | collective-permute-start | bytes 122888 | tf_op jit(solution)/shard_map/ppermute | solution.py:24
  96.7 23.4 %copy-start.15 = (f32[5,16,31,128]{3,1,0,2:T(8,128)S(1)}, f32[5,16,31,128]{3,1,0,2:T(8,128)}, u32[]{:S(2)}) copy-start(f32[5,16,31,128]{3,1,0,2:T(8,128)} %get-tuple-element.123) | copy-start | bytes 3809284
  135.4 11.5 %collective-permute-start.10 = (f32[5,16,1,128]{3,1,0,2:T(8,128)S(1)}, f32[5,16,1,128]{3,1,0,2:T(8,128)S(1)}, u32[]{:S(2)}, u32[]{:S(2)}) collective-permute-start(f32[5,16,1,128]{3,1,0,2:T(8,128)S(1)} %bitcast.205), channel_id=1, source_target_pairs={{0,1},{1,2},{2,3},{3,4},{4,5},{5,6},{6,7},{8,9},{9,10},{10,11},{11... | collective-permute-start | bytes 122888 | tf_op jit(solution)/shard_map/ppermute | solution.py:22
  139.9 7.1 %collective-permute-start.11 = (f32[5,16,1,128]{3,1,0,2:T(8,128)S(1)}, f32[5,16,1,128]{3,1,0,2:T(8,128)S(1)}, u32[]{:S(2)}, u32[]{:S(2)}) collective-permute-start(f32[5,16,1,128]{3,1,0,2:T(8,128)S(1)} %bitcast.204), channel_id=1, source_target_pairs={{1,0},{2,1},{3,2},{4,3},{5,4},{6,5},{7,6},{9,8},{10,9},{11,10},{12... | collective-permute-start | bytes 122888 | tf_op jit(solution)/shard_map/ppermute | solution.py:24
  145.1 26.9 %collective-permute-start.8 = (f32[5,1,32,128]{3,2,1,0:T(8,128)S(1)}, f32[5,1,32,128]{3,2,1,0:T(8,128)S(1)}, u32[]{:S(2)}, u32[]{:S(2)}) collective-permute-start(f32[5,1,32,128]{3,2,1,0:T(8,128)S(1)} %get-tuple-element.114), channel_id=1, source_target_pairs={{8,0},{16,8},{24,16},{32,24},{40,32},{48,40},{56,48},{64,56},{72,6... | collective-permute-start | bytes 245768 | tf_op jit(solution)/shard_map/ppermute | solution.py:24
  145.6 26.4 %collective-permute-start.9 = (f32[5,1,32,128]{3,2,1,0:T(8,128)S(1)}, f32[5,1,32,128]{3,2,1,0:T(8,128)S(1)}, u32[]{:S(2)}, u32[]{:S(2)}) collective-permute-start(f32[5,1,32,128]{3,2,1,0:T(8,128)S(1)} %get-tuple-element.113), channel_id=1, source_target_pairs={{0,8},{8,16},{16,24},{24,32},{32,40},{40,48},{48,56},{56,64},{64,7... | collective-permute-start | bytes 245768 | tf_op jit(solution)/shard_map/ppermute | solution.py:22
  182.2 11.1 %copy-start.34 = (f32[16,32]{1,0:T(8,128)S(1)}, f32[16,32]{1,0:T(8,128)}, u32[]{:S(2)}) copy-start(f32[16,32]{1,0:T(8,128)} %get-tuple-element.66) | copy-start | bytes 6148
  182.2 11.2 %copy-start.35 = (pred[128,4]{0,1:T(4,128)(4,1)S(1)}, pred[128,4]{0,1:T(4,128)(4,1)}, u32[]{:S(2)}) copy-start(pred[128,4]{0,1:T(4,128)(4,1)} %iota_compare_fusion.3) | copy-start | bytes 1540
  182.2 12.5 %copy-start.33 = (f32[16,32]{1,0:T(8,128)S(1)}, f32[16,32]{1,0:T(8,128)}, u32[]{:S(2)}) copy-start(f32[16,32]{1,0:T(8,128)} %get-tuple-element.68) | copy-start | bytes 6148
  184.9 55.6 %all-to-all-start = ((f32[128,4,128]{2,1,0:T(4,128)}), f32[128,4,128]{2,1,0:T(4,128)}, u32[]{:S(2)}, u32[]{:S(2)}) async-start(f32[128,4,128]{2,1,0:T(4,128)} %copy.296), calls=%async_computation | async-start | bytes 524288 | tf_op jit(solution)/shard_map/all_to_all | solution.py:148
  197.4 55.8 %collective-permute-start.12 = (f32[5,1,32,128]{3,2,1,0:T(8,128)}, f32[5,1,32,128]{3,2,1,0:T(8,128)}, u32[]{:S(2)}, u32[]{:S(2)}) collective-permute-start(f32[5,1,32,128]{3,2,1,0:T(8,128)} %get-tuple-element.106), channel_id=1, source_target_pairs={{8,0},{16,8},{24,16},{32,24},{40,32},{48,40},{56,48},{64,56},{72,6... | collective-permute-start | bytes 245768 | tf_op jit(solution)/shard_map/ppermute | solution.py:24
  198.5 54.7 %collective-permute-start.13 = (f32[5,1,32,128]{3,2,1,0:T(8,128)}, f32[5,1,32,128]{3,2,1,0:T(8,128)}, u32[]{:S(2)}, u32[]{:S(2)}) collective-permute-start(f32[5,1,32,128]{3,2,1,0:T(8,128)} %get-tuple-element.105), channel_id=1, source_target_pairs={{0,8},{8,16},{16,24},{24,32},{32,40},{40,48},{48,56},{56,64},{64,7... | collective-permute-start | bytes 245768 | tf_op jit(solution)/shard_map/ppermute | solution.py:22
  199.3 14.2 %collective-permute-start.14 = (f32[5,16,1,128]{3,1,0,2:T(8,128)S(1)}, f32[5,16,1,128]{3,1,0,2:T(8,128)S(1)}, u32[]{:S(2)}, u32[]{:S(2)}) collective-permute-start(f32[5,16,1,128]{3,1,0,2:T(8,128)S(1)} %copy.400), channel_id=1, source_target_pairs={{0,1},{1,2},{2,3},{3,4},{4,5},{5,6},{6,7},{8,9},{9,10},{10,11},{11... | collective-permute-start | bytes 122888 | tf_op jit(solution)/shard_map/ppermute | solution.py:22
  202.6 10.9 %collective-permute-start.15 = (f32[5,16,1,128]{3,1,0,2:T(8,128)S(1)}, f32[5,16,1,128]{3,1,0,2:T(8,128)S(1)}, u32[]{:S(2)}, u32[]{:S(2)}) collective-permute-start(f32[5,16,1,128]{3,1,0,2:T(8,128)S(1)} %copy.399), channel_id=1, source_target_pairs={{1,0},{2,1},{3,2},{4,3},{5,4},{6,5},{7,6},{9,8},{10,9},{11,10},{12... | collective-permute-start | bytes 122888 | tf_op jit(solution)/shard_map/ppermute | solution.py:24
  213.5 25.6 %copy-start.11 = (f32[5,16,31,128]{3,2,1,0:T(8,128)}, f32[5,16,31,128]{3,2,1,0:T(8,128)S(1)}, u32[]{:S(2)}) copy-start(f32[5,16,31,128]{3,2,1,0:T(8,128)S(1)} %get-tuple-element.107) | copy-start | bytes 3809284
  213.5 25.6 %copy-start.12 = (f32[5,16,31,128]{3,2,1,0:T(8,128)}, f32[5,16,31,128]{3,2,1,0:T(8,128)S(1)}, u32[]{:S(2)}) copy-start(f32[5,16,31,128]{3,2,1,0:T(8,128)S(1)} %get-tuple-element.108) | copy-start | bytes 3809284
  240.5 17.7 %all-to-all-start.1 = ((f32[128,4,128]{2,1,0:T(4,128)}), f32[128,4,128]{2,1,0:T(4,128)}, u32[]{:S(2)}, u32[]{:S(2)}) async-start(f32[128,4,128]{2,1,0:T(4,128)} %copy.298), calls=%async_computation.1 | async-start | bytes 524288 | tf_op jit(solution)/shard_map/all_to_all | solution.py:148
  258.2 17.9 %all-to-all-start.2 = ((f32[128,4,128]{2,1,0:T(4,128)}), f32[128,4,128]{2,1,0:T(4,128)}, u32[]{:S(2)}, u32[]{:S(2)}) async-start(f32[128,4,128]{2,1,0:T(4,128)} %copy.299), calls=%async_computation.2 | async-start | bytes 524288 | tf_op jit(solution)/shard_map/all_to_all | solution.py:148
  276.1 16.0 %all-to-all-start.3 = ((f32[128,4,128]{2,1,0:T(4,128)}), f32[128,4,128]{2,1,0:T(4,128)}, u32[]{:S(2)}, u32[]{:S(2)}) async-start(f32[128,4,128]{2,1,0:T(4,128)} %copy.300), calls=%async_computation.3 | async-start | bytes 524288 | tf_op jit(solution)/shard_map/all_to_all | solution.py:148
  (29 other events, 67.3 us)
where the time goes:
time: 356 us; the launch traced here: 349 us
  blocking collectives  94.7 us (27%)
  matrix products  91.4 us (26%)
  starting transfers between devices  59 us (17%)
  other arithmetic  49.3 us (14%)
  local copies, waits for them, and re-layouts  36.1 us (10%)
  waiting for transfers between devices  10.8 us (3%)
  between operations  7.29 us (2%)
    all_gather x4, blocking collectives, roll_gathered(): gathered = lax.all_gather(interface_row, 'sector', axis=1, tiled=True)  94.7 us
    dot_general x2, matrix products, one_observer(): jnp.einsum('mb,mw->wb', selector, weights, precision=lax.Precision.HIGHEST)  50.4 us
    dot_general x12, matrix products, apply_jacobian(): jnp.einsum('ij,jtzr->itzr', matrix, flow_field, precision=lax.Precision.H...  38.9 us
    all_to_all x4, starting transfers between devices, record(): lax.all_to_all(parcel, ('sector', 'axial'), split_axis=0, concat_axis=0,...  29.2 us
    ppermute x8, starting transfers between devices, with_halo(): lax.ppermute(tail, axis, [(i, (i + 1) % count) for i in range(ends)])  20.9 us
    all_to_all x4, waiting for transfers between devices, record(): lax.all_to_all(parcel, ('sector', 'axial'), split_axis=0, concat_axis=0,...  10.8 us
    unnamed x88, local copies, waits for them, and re-layouts  10.1 us
    ppermute x8, starting transfers between devices, with_halo(): lax.ppermute(head, axis, [((i + 1) % count, i) for i in range(ends)])  8.81 us
  transfers between devices with their start and end apart: 20, of which 3 were waited for; matrix products, arithmetic and copies ran while one was open for 23% of the time, Pallas kernels for 0%

commit v1 on v0

v1 whole, which is shorter than its diff:
```python
import jax
import jax.numpy as jnp
from jax import lax
from jax.experimental import pallas as pl
from jax.experimental.pallas import tpu as pltpu
from jax.sharding import PartitionSpec as P

NV = 5
NA = 16
NB = 8
CT = 16
CZ = 32
NR = 128
ROWS = CT * CZ
PAD = ROWS + 2 * CZ
NBIN = 128
PIECE = 8

time_step = 0.3
viscosity = 0.05

MESH = pl.DeviceIdType.MESH


def wait_rows(ref, sem):
    pltpu.make_async_copy(ref, ref, sem).wait()


def step_kernel(
    x_ref,
    damp_ref,
    jac_ref,
    fw_ref,
    shift_ref,
    list_ref,
    new_ref,
    gather_ref,
    s1,
    s2,
    s3,
    s4,
    edge_lo,
    edge_hi,
    ghost_lo,
    ghost_hi,
    row_out,
    row_sel,
    held1,
    held2,
    held3,
    held4,
    in1,
    in2,
    in3,
    in4,
    window,
    parcel,
    load_sem,
    theta_send,
    theta_recv,
    axial_send,
    axial_recv,
    row_send,
    row_recv,
    sel_send,
    sel_recv,
    ring_send,
    ring_recv,
    line_send,
    line_recv,
):
    a = lax.axis_index("sector")
    b = lax.axis_index("axial")
    front = b == NB // 2 - 1
    aft = b == NB // 2
    interface = jnp.logical_or(front, aft)
    other = jnp.where(front, NB // 2, NB // 2 - 1)
    has_lo = jnp.logical_and(b > 0, jnp.logical_not(aft))
    has_hi = jnp.logical_and(b < NB - 1, jnp.logical_not(front))
    states = [s1, s2, s3, s4]
    row_held = [held1, held2, held3, held4]
    row_in = [in1, in2, in3, in4]

    load = pltpu.make_async_copy(x_ref, s1.at[:, pl.ds(CZ, ROWS), :], load_sem.at[0])
    load.start()

    barrier = pltpu.get_barrier_semaphore()

    @pl.loop(1, NA)
    def _(step):
        pl.semaphore_signal(barrier, inc=1, device_id=(lax.rem(a + step, NA), b), device_id_type=MESH)

    @pl.loop(1, NB)
    def _(step):
        pl.semaphore_signal(barrier, inc=1, device_id=(a, lax.rem(b + step, NB)), device_id_type=MESH)

    @pl.when(interface)
    def _():
        @pl.loop(0, NA)
        def _(step):
            pl.semaphore_signal(barrier, inc=1, device_id=(step, other), device_id_type=MESH)

    row_out[...] = jnp.zeros_like(row_out)
    parcel[...] = jnp.zeros_like(parcel)
    for k in range(4):
        @pl.when(b == 0)
        def _():
            ghost_lo[k] = jnp.zeros((NV, CT, NR), jnp.float32)

        @pl.when(b == NB - 1)
        def _():
            ghost_hi[k] = jnp.zeros((NV, CT, NR), jnp.float32)

    pl.semaphore_wait(barrier, jnp.where(interface, NA - 1 + NB - 1 + NA, NA - 1 + NB - 1))

    def ring_start(which):
        slot = pl.multiple_of((b * NA + a) * PIECE, PIECE)
        gather_ref[which, pl.ds(slot, PIECE), :] = parcel[which]

        @pl.loop(1, NA)
        def _(step):
            pltpu.make_async_remote_copy(
                src_ref=parcel.at[which],
                dst_ref=gather_ref.at[which, pl.ds(slot, PIECE), :],
                send_sem=ring_send.at[which],
                recv_sem=ring_recv.at[which],
                device_id=(lax.rem(a + step, NA), b),
                device_id_type=MESH,
            ).start()

    def line_start(which):
        wait_rows(gather_ref.at[which, pl.ds(0, (NA - 1) * PIECE), :], ring_recv.at[which])
        slot = pl.multiple_of(b * NA * PIECE, NA * PIECE)

        @pl.loop(1, NB)
        def _(step):
            pltpu.make_async_remote_copy(
                src_ref=gather_ref.at[which, pl.ds(slot, NA * PIECE), :],
                dst_ref=gather_ref.at[which, pl.ds(slot, NA * PIECE), :],
                send_sem=line_send.at[which],
                recv_sem=line_recv.at[which],
                device_id=(a, lax.rem(b + step, NB)),
                device_id_type=MESH,
            ).start()

    def line_wait(which):
        wait_rows(gather_ref.at[which, pl.ds(0, (NB - 1) * NA * PIECE), :], line_recv.at[which])

    def theta_copies(k):
        state = states[k]
        down = pltpu.make_async_remote_copy(
            src_ref=state.at[:, pl.ds(CZ, CZ), :],
            dst_ref=state.at[:, pl.ds(CZ + ROWS, CZ), :],
            send_sem=theta_send.at[k, 0],
            recv_sem=theta_recv.at[k, 0],
            device_id=(lax.rem(a + NA - 1, NA), b),
            device_id_type=MESH,
        )
        up = pltpu.make_async_remote_copy(
            src_ref=state.at[:, pl.ds(ROWS, CZ), :],
            dst_ref=state.at[:, pl.ds(0, CZ), :],
            send_sem=theta_send.at[k, 1],
            recv_sem=theta_recv.at[k, 1],
            device_id=(lax.rem(a + 1, NA), b),
            device_id_type=MESH,
        )
        return down, up

    def axial_copies(k):
        down = pltpu.make_async_remote_copy(
            src_ref=edge_lo.at[k],
            dst_ref=ghost_hi.at[k],
            send_sem=axial_send.at[k, 0],
            recv_sem=axial_recv.at[k, 0],
            device_id=(a, jnp.maximum(b - 1, 0)),
            device_id_type=MESH,
        )
        up = pltpu.make_async_remote_copy(
            src_ref=edge_hi.at[k],
            dst_ref=ghost_lo.at[k],
            send_sem=axial_send.at[k, 1],
            recv_sem=axial_recv.at[k, 1],
            device_id=(a, jnp.minimum(b + 1, NB - 1)),
            device_id_type=MESH,
        )
        return down, up

    def send_edges(k):
        state = states[k]

        @pl.when(front)
        def _():
            for v in range(NV):
                row_out[k, pl.ds(v, CT, stride=PIECE), :] = state[v, pl.ds(CZ + CZ - 1, CT, stride=CZ), :]

        @pl.when(aft)
        def _():
            for v in range(NV):
                row_out[k, pl.ds(v, CT, stride=PIECE), :] = state[v, pl.ds(CZ, CT, stride=CZ), :]

        @pl.when(interface)
        def _():
            @pl.loop(0, CT)
            def _(t):
                pltpu.make_async_remote_copy(
                    src_ref=row_out.at[k, pl.ds(pl.multiple_of(t * PIECE, PIECE), PIECE), :],
                    dst_ref=row_held[k].at[a],
                    send_sem=row_send.at[k],
                    recv_sem=row_recv.at[k],
                    device_id=(t, other),
                    device_id_type=MESH,
                ).start()

        down, up = theta_copies(k)
        down.start()
        up.start()
        down, up = axial_copies(k)

        @pl.when(has_lo)
        def _():
            for v in range(NV):
                edge_lo[k, v] = state[v, pl.ds(CZ, CT, stride=CZ), :]
            down.start()

        @pl.when(has_hi)
        def _():
            for v in range(NV):
                edge_hi[k, v] = state[v, pl.ds(CZ + CZ - 1, CT, stride=CZ), :]
            up.start()

    def turn(k):
        r = shift_ref[k]
        return jnp.where(front, r, (CT * NA - r) & (CT * NA - 1))

    def relay(k):
        @pl.when(interface)
        def _():
            wait_rows(row_held[k], row_recv.at[k])
            first = (turn(k) - a + CT - 1) >> 4

            @pl.loop(0, NA)
            def _(d):
                row_sel[k, d] = row_held[k][(d + first) & (NA - 1)]

            @pl.loop(1, NA)
            def _(step):
                d = lax.rem(a + step, NA)
                pltpu.make_async_remote_copy(
                    src_ref=row_sel.at[k, d],
                    dst_ref=row_in[k].at[a],
                    send_sem=sel_send.at[k],
                    recv_sem=sel_recv.at[k],
                    device_id=(d, b),
                    device_id_type=MESH,
                ).start()
            row_in[k][a] = row_sel[k, a]

    def land(k):
        @pl.when(interface)
        def _():
            wait_rows(row_in[k].at[pl.ds(0, NA - 1)], sel_recv.at[k])
            r = turn(k)
            for t in range(CT):
                window[pl.ds(t * PIECE, PIECE), :] = row_in[k][(r + t) & (CT - 1)]

        @pl.when(front)
        def _():
            for v in range(NV):
                ghost_hi[k, v] = window[pl.ds(v, CT, stride=PIECE), :]

        @pl.when(aft)
        def _():
            for v in range(NV):
                ghost_lo[k, v] = window[pl.ds(v, CT, stride=PIECE), :]

        down, up = axial_copies(k)

        @pl.when(has_hi)
        def _():
            down.wait_recv()

        @pl.when(has_lo)
        def _():
            up.wait_recv()

    lane = lax.broadcasted_iota(jnp.int32, (CZ, NR), 1)
    line = lax.broadcasted_iota(jnp.int32, (CZ, NR), 0)

    def plane(k, t):
        state = states[k]
        base = pl.multiple_of(t * CZ, CZ)
        here = pl.ds(pl.multiple_of(base + CZ, CZ), CZ)
        center = [state[v, here, :] for v in range(NV)]
        advection = [None] * NV
        total = [None] * NV
        for d in range(3):
            for j in range(NV):
                c = center[j]
                if d == 0:
                    upper = state[j, pl.ds(pl.multiple_of(base + 2 * CZ, CZ), CZ), :]
                    lower = state[j, pl.ds(base, CZ), :]
                elif d == 1:
                    upper = jnp.where(line == CZ - 1, 0.0, pltpu.roll(c, CZ - 1, 0))
                    lower = jnp.where(line == 0, 0.0, pltpu.roll(c, 1, 0))
                else:
                    upper = jnp.where(lane == NR - 1, 0.0, pltpu.roll(c, NR - 1, 1))
                    lower = jnp.where(lane == 0, 0.0, pltpu.roll(c, 1, 1))
                both = upper + lower
                total[j] = both if d == 0 else total[j] + both
                slope = upper - lower
                for i in range(NV):
                    term = (0.5 * jac_ref[d, i, j]) * slope
                    advection[i] = term if advection[i] is None else advection[i] + term
        drag = damp_ref[pl.ds(base, CZ), :] + 6.0 * viscosity
        for i in range(NV):
            rate = viscosity * total[i] - advection[i] - drag * center[i]
            start = s1[i, here, :] if k else center[i]
            if k < 3:
                scale = time_step if k == 2 else 0.5 * time_step
                states[k + 1][i, here, :] = start + scale * rate
            else:
                mix = (s2[i, here, :] + 2.0 * s3[i, here, :] + center[i] - start) * (1.0 / 3.0)
                new_ref[i, pl.ds(base, CZ), :] = mix + (time_step / 6.0) * rate

    def correct(k):
        for side, ghost in ((0, ghost_lo), (1, ghost_hi)):
            sign = 0.5 if side == 0 else -0.5
            row = 0 if side == 0 else CZ - 1
            values = [ghost[k, j] for j in range(NV)]
            for i in range(NV):
                rate = viscosity * values[i]
                for j in range(NV):
                    rate = rate + (sign * jac_ref[1, i, j]) * values[j]
                if k < 3:
                    scale = time_step if k == 2 else 0.5 * time_step
                    where = pl.ds(CZ + row, CT, stride=CZ)
                    states[k + 1][i, where, :] = states[k + 1][i, where, :] + scale * rate
                else:
                    where = pl.ds(row, CT, stride=CZ)
                    new_ref[i, where, :] = new_ref[i, where, :] + (time_step / 6.0) * rate

    pick = (lax.broadcasted_iota(jnp.int32, (8, NR), 1) == NR // 2).astype(jnp.float32)

    def sample(k):
        state = states[k]
        total = None
        for v in range(NV):
            column = lax.dot_general(
                pick,
                state[v, pl.ds(CZ, ROWS), :],
                (((1,), (1,)), ((), ())),
                precision=lax.Precision.HIGHEST,
                preferred_element_type=jnp.float32,
            )
            term = column[0:1] * fw_ref[v]
            total = term if total is None else total + term
        for block in range(4):
            row = 2 * block + k % 2
            parcel[1 + k // 2, row : row + 1, :] = total[:, block * 128 : (block + 1) * 128]

    parcel[0] = list_ref[...]
    ring_start(0)
    load.wait()
    send_edges(0)
    for k in range(4):
        @pl.loop(1, CT // 2)
        def _(t):
            plane(k, t)

        relay(k)

        @pl.loop(CT // 2, CT - 1)
        def _(t):
            plane(k, t)

        if k == 0:
            sample(0)
            line_start(0)
        elif k == 1:
            sample(1)
            ring_start(1)
        elif k == 2:
            line_start(1)
            sample(2)
        else:
            line_start(2)
        down, up = theta_copies(k)
        down.wait_recv()
        up.wait_recv()

        @pl.loop(0, 2)
        def _(side):
            plane(k, side * (CT - 1))

        land(k)
        correct(k)
        if k < 3:
            send_edges(k + 1)
        if k == 2:
            sample(3)
            ring_start(2)

    for which in range(3):
        line_wait(which)
        wait_rows(gather_ref.at[which, pl.ds(0, (NA - 1) * PIECE), :], ring_send.at[which])
        wait_rows(gather_ref.at[which, pl.ds(0, (NB - 1) * NA * PIECE), :], line_send.at[which])
    for k in range(4):
        down, up = theta_copies(k)
        down.wait_send()
        up.wait_send()
        down, up = axial_copies(k)

        @pl.when(has_lo)
        def _():
            down.wait_send()

        @pl.when(has_hi)
        def _():
            up.wait_send()

        @pl.when(interface)
        def _():
            wait_rows(row_out.at[k], row_send.at[k])
            wait_rows(row_sel.at[k, pl.ds(0, NA - 1)], sel_send.at[k])


def step_call(x, damping, jacobians, face_weight, phase_shift, lists):
    vmem = pl.BlockSpec(memory_space=pltpu.VMEM)
    smem = pl.BlockSpec(memory_space=pltpu.SMEM)
    state = pltpu.VMEM((NV, PAD, NR), jnp.float32)
    edge = pltpu.VMEM((4, NV, CT, NR), jnp.float32)
    row = pltpu.VMEM((4, CT * PIECE, NR), jnp.float32)
    held = pltpu.VMEM((NA, PIECE, NR), jnp.float32)
    dma = pltpu.SemaphoreType.DMA
    return pl.pallas_call(
        step_kernel,
        out_shape=(
            jax.ShapeDtypeStruct((NV, ROWS, NR), jnp.float32),
            jax.ShapeDtypeStruct((3, NA * NB * PIECE, NR), jnp.float32),
        ),
        in_specs=[pl.BlockSpec(memory_space=pl.ANY), vmem, smem, vmem, smem, vmem],
        out_specs=(vmem, vmem),
        scratch_shapes=[state] * 4
        + [edge] * 4
        + [row, pltpu.VMEM((4, NA, PIECE, NR), jnp.float32)]
        + [held] * 8
        + [pltpu.VMEM((CT * PIECE, NR), jnp.float32), pltpu.VMEM((3, PIECE, NR), jnp.float32)]
        + [dma((1,)), dma((4, 2)), dma((4, 2)), dma((4, 2)), dma((4, 2))]
        + [dma((4,))] * 4
        + [dma((3,))] * 4,
        compiler_params=pltpu.CompilerParams(
            collective_id=0, has_side_effects=True, vmem_limit_bytes=40 << 20
        ),
        name="substeps",
    )(x, damping, jacobians, face_weight, phase_shift, lists)


def bin_kernel(list_ref, bin_ref, fraction_ref, gain_ref, early_ref, late_ref, out_ref, total):
    step = pl.program_id(0)

    @pl.when(step == 0)
    def _():
        total[...] = jnp.zeros_like(total)

    place = lax.broadcasted_iota(jnp.int32, (8, 128), 0)
    low = place < 4
    sample = place % 4
    sign = jnp.where(low, -1.0, 1.0).astype(jnp.float32)
    shift = jnp.where(low, 1.0, 0.0).astype(jnp.float32)
    fine = lax.broadcasted_iota(jnp.int32, (32, 128), 0).astype(jnp.float32).astype(jnp.bfloat16)
    zero = jnp.zeros((16, 128), jnp.bfloat16)

    def spread(ref, row):
        return jnp.broadcast_to(ref[row : row + 1], (8, 128))

    for a in range(NA):
        gain = gain_ref[a, 0]
        fraction = fraction_ref[a, 0]
        bins = bin_ref[a, 0]
        coarse_bin = (bins >> 5).astype(jnp.float32)
        fine_bin = (bins & 31).astype(jnp.float32)
        early = early_ref[0, 0, a]
        late = late_ref[0, 0, a]
        lists = list_ref[0, 0, a]
        blocks = []
        for block in range(4):
            later = jnp.where(sample == 2, spread(late, 2 * block), spread(late, 2 * block + 1))
            later = jnp.where(sample == 1, spread(early, 2 * block + 1), later)
            blocks.append(jnp.where(sample == 0, spread(early, 2 * block), later))
        count = spread(lists, 4)
        weights = [[], []]
        selectors = [[], []]
        for c in range(4):
            listed = spread(lists, c)
            received = jnp.zeros((8, 128), jnp.float32)
            for block in range(4):
                received = jnp.where(listed == block, blocks[block], received)
            received = jnp.where(count > c, received, 0.0)
            for o in range(2):
                row = 2 * c + o
                part = received * (spread(gain, row) * (spread(fraction, row) * sign + shift))
                head = part.astype(jnp.bfloat16).astype(jnp.float32)
                both = jnp.concatenate([head, part - head], 0).astype(jnp.bfloat16)
                coarse = jnp.broadcast_to(coarse_bin[row : row + 1], (16, 128)).astype(jnp.bfloat16)
                weights[o].append(
                    jnp.concatenate([jnp.where(coarse == jnp.bfloat16(q), both, zero) for q in range(4)], 0)
                )
                within = jnp.broadcast_to(fine_bin[row : row + 1], (32, 128)).astype(jnp.bfloat16)
                selectors[o].append(jnp.where(within == fine, jnp.bfloat16(1), jnp.bfloat16(0)))
        for o in range(2):
            total[o] += lax.dot_general(
                jnp.concatenate(weights[o], 1),
                jnp.concatenate(selectors[o], 1),
                (((1,), (1,)), ((), ())),
                preferred_element_type=jnp.float32,
            )

    @pl.when(step == pl.num_programs(0) - 1)
    def _():
        for o in range(2):
            signal = jnp.zeros((1, NBIN), jnp.float32)
            for q in range(8):
                offset = q % 4 + q // 4
                pieces = [
                    total[o, 16 * g + q : 16 * g + q + 1, :] + total[o, 16 * g + 8 + q : 16 * g + 9 + q, :]
                    for g in range(4)
                ]
                whole = jnp.concatenate(pieces, 1)
                signal = signal + (pltpu.roll(whole, offset, 1) if offset else whole)
            out_ref[o : o + 1, :] = signal


def bin_call(gathered, lists, bins, fractions, gains):
    owned = pl.BlockSpec((NA, 1, PIECE, 128), lambda s: (0, s, 0, 0))

    def part(which):
        return pl.BlockSpec((1, 1, NA, PIECE, 128), lambda s: (which, s, 0, 0, 0))

    return pl.pallas_call(
        bin_kernel,
        grid=(NB,),
        in_specs=[part(0), owned, owned, owned, part(1), part(2)],
        out_specs=pl.BlockSpec((2, NBIN), lambda s: (0, 0)),
        out_shape=jax.ShapeDtypeStruct((2, NBIN), jnp.float32),
        scratch_shapes=[pltpu.VMEM((2, 64, 32), jnp.float32)],
        compiler_params=pltpu.CompilerParams(vmem_limit_bytes=40 << 20),
        name="binning",
    )(lists, bins, fractions, gains, gathered, gathered)


def local(
    flow_state,
    damping,
    jacobians,
    face_weight,
    phase_shift,
    face_list,
    face_count,
    arrival_bin,
    arrival_fraction,
    arrival_gain,
):
    lists = jnp.concatenate(
        [face_list[0].T, face_count, jnp.zeros((3, NA * NB), jnp.int32)], axis=0
    ).astype(jnp.float32)
    new_state, gathered = step_call(
        flow_state.reshape(NV, ROWS, NR),
        damping.reshape(ROWS, NR),
        jacobians,
        face_weight.reshape(NV, 1, ROWS),
        phase_shift,
        lists,
    )
    owner = lax.axis_index("sector") * NB + lax.axis_index("axial")
    mine = lax.dynamic_slice_in_dim(gathered[0], owner, 1, axis=1)
    lists = jnp.broadcast_to(mine, (NA * NB * PIECE, NR)).reshape(1, NB, NA, PIECE, NR)
    signal = bin_call(
        gathered.reshape(3, NB, NA, PIECE, NR),
        lists,
        arrival_bin.reshape(NA, NB, PIECE, 128),
        arrival_fraction.reshape(NA, NB, PIECE, 128),
        arrival_gain.reshape(NA, NB, PIECE, 128),
    )
    return new_state.reshape(NV, CT, CZ, NR), signal


def solution(mesh):
    return jax.shard_map(
        local,
        mesh=mesh,
        in_specs=(
            P(None, "sector", "axial", None),
            P("sector", "axial", None),
            P(),
            P(None, "sector", "axial"),
            P(),
            P(("sector", "axial"), None, None),
            P(("sector", "axial"), None),
            P(("sector", "axial"), None, None, None, None),
            P(("sector", "axial"), None, None, None, None),
            P(("sector", "axial"), None, None, None, None),
        ),
        out_specs=(P(None, "sector", "axial", None), P(("sector", "axial"), None)),
        check_vma=False,
    )
```

time: 356 us -> 75.7 us (0.21); the launches traced: 349 us -> 75.2 us
  blocking collectives: 94.7 us -> 0 us
  matrix products: 91.4 us -> 0 us
  Pallas kernels: 0 us -> 65 us
  starting transfers between devices: 59 us -> 0 us
  other arithmetic: 49.3 us -> 0.77 us
  local copies, waits for them, and re-layouts: 36.1 us -> 8.71 us
  waiting for transfers between devices: 10.8 us -> 0 us
  between operations: 7.29 us -> 0.7 us
    all_gather x4 -> x0, blocking collectives: 94.7 us -> none  [roll_gathered(): gathered = lax.all_gather(interface_row, 'sector', axis=1, tiled=True)]
    dot_general x18 -> x0, matrix products: 91.4 us -> none  [the longest x2 50.4 us: one_observer(): jnp.einsum('mb,mw->wb', selector, weights, precision=lax.Precision.HIGHEST)]
    pallas_call x0 -> x2, Pallas kernels: none -> 65 us  [the longest x1 57.9 us: step_call(): pl.pallas_call(step_kernel, out_shape=(jax.ShapeDtypeStruct((NV, ROWS, NR...]
    ppermute x16 -> x0, starting transfers between devices: 29.7 us -> none  [the longest x8 20.9 us: with_halo(): lax.ppermute(tail, axis, [(i, (i + 1) % count) for i in range(ends)])]
    all_to_all x4 -> x0, starting transfers between devices: 29.2 us -> none  [record(): lax.all_to_all(parcel, ('sector', 'axial'), split_axis=0, concat_axis=0,...]
    add x6 -> x0, other arithmetic: 21 us -> none  [the longest x1 7.34 us: local(): flow_state + time_step / 6.0 * (rate_one + 2.0 * rate_two + 2.0 * rate_th...]
    mul x16 -> x0, other arithmetic: 19.7 us -> none  [the longest x4 4.74 us: tendency(): 0.5 * (axial_plus - axial_minus)]
    slice x33 -> x1, local copies, waits for them, and re-layouts: 19.4 us -> 0.04 us  [local(): mine = lax.dynamic_slice_in_dim(gathered[0], owner, 1, axis=1)]
  transfers between devices with their start and end apart: 20 -> 0, of which waited for: 3 -> 0; matrix products, arithmetic and copies ran while one was open for 23% -> 0% of each run, Pallas kernels for 0% -> 0%
where the time goes in v1:
time: 75.7 us; the launch traced here: 75.2 us
  Pallas kernels  65 us (86%)
  local copies, waits for them, and re-layouts  8.71 us (12%)
  other arithmetic  0.77 us (1%)
    pallas_call x1, Pallas kernels, step_call(): pl.pallas_call(step_kernel, out_shape=(jax.ShapeDtypeStruct((NV, ROWS, NR...  57.9 us
    pallas_call x1, Pallas kernels, bin_call(): pl.pallas_call(bin_kernel, grid=(NB,), in_specs=[part(0), owned, owned, o...  7.1 us
    unnamed x14, local copies, waits for them, and re-layouts  7.09 us

profile of v1, /device:TPU:1, one launch (start us, length us, event | category | flops | bytes accessed | tf_op | source)
XLA Modules:
  0.0 75.2 jit_solution(4897935341866828785)
XLA Ops:
  0.6 0.7 copy.13.jac_ref
  1.3 0.9 %reshape.38.fw_ref = f32[5,1,512]{2,1,0:T(1,128)S(1)} reshape(f32[5,16,32]{2,1,0:T(8,128)} %param.13) | data formatting | bytes 20480 | tf_op jit(solution)/shard_map/reshape | solution.py:570
  2.2 0.1 pad.2.clone
  2.3 0.8 %add_convert_fusion.list_ref = f32[8,128]{1,0:T(8,128)S(1)} fusion(s32[1,128]{1,0:T(1,128)} %param.16, s32[4,128]{1,0:T(4,128)} %bitcast.18, s32[8]{0:T(128)S(1)} %pad.2.clone), kind=kLoop, calls=%fused_computation.1 | loop fusion | flops 3072 | bytes 6688 | tf_op jit(solution)/shard_map/convert_element_type | solution.py:565
  3.1 0.0 copy-start
  3.1 1.3 %copy-done = f32[5,16,32,128]{3,2,1,0:T(8,128)S(1)} copy-done((f32[5,16,32,128]{3,2,1,0:T(8,128)S(1)}, f32[5,16,32,128]{3,2,1,0:T(8,128)}, u32[]{:S(2)}) %copy-start) | copy-done | bytes 1310744
  4.4 0.0 copy-start.4
  4.4 0.9 %copy-done.4 = f32[16,32,128]{2,1,0:T(8,128)S(1)} copy-done((f32[16,32,128]{2,1,0:T(8,128)S(1)}, f32[16,32,128]{2,1,0:T(8,128)}, u32[]{:S(2)}) %copy-start.4) | copy-done | bytes 262168
  5.3 0.0 copy-start.5
  5.3 0.7 copy-done.5
  6.0 57.9 %substeps.1 = (f32[5,512,128]{2,1,0:T(8,128)S(1)}, f32[3,1024,128]{2,1,0:T(8,128)S(1)}) custom-call(f32[5,512,128]{2,1,0:T(8,128)S(1)} %bitcast.12, f32[512,128]{1,0:T(8,128)S(1)} %bitcast.17, f32[3,5,5]{2,1,0:T(8,128)S(1)} %copy.13.jac_ref, f32[5,1,512]{2,1,0:T(1,128)S(1)} %reshape.38.fw_ref, s32[4]{0:T(128)S(1)} %copy-done.5, ...), custom_call_target="tpu_custom_call" | custom-call | tf_op jit(solution)/shard_map/substeps/pallas_call | solution.py:435
  63.9 0.0 copy-start.1
  64.0 0.4 dynamic-slice_reduce_fusion
  64.3 0.1 broadcast_in_dim.11
  64.4 0.2 broadcast_in_dim.12.list_ref
  64.6 0.3 copy-done.1
  64.9 0.0 copy-start.2
  64.9 1.0 %copy-done.2 = f32[1,128,4,2,128]{4,3,2,1,0:T(2,128)S(1)} copy-done((f32[1,128,4,2,128]{4,3,2,1,0:T(2,128)S(1)}, f32[1,128,4,2,128]{4,3,2,1,0:T(2,128)}, u32[]{:S(2)}) %copy-start.2) | copy-done | bytes 524312
  66.0 0.0 copy-start.3
  66.0 1.0 %copy-done.3 = f32[1,128,4,2,128]{4,3,2,1,0:T(2,128)S(1)} copy-done((f32[1,128,4,2,128]{4,3,2,1,0:T(2,128)S(1)}, f32[1,128,4,2,128]{4,3,2,1,0:T(2,128)}, u32[]{:S(2)}) %copy-start.3) | copy-done | bytes 524312
  67.0 7.1 %binning.1 = f32[2,128]{1,0:T(2,128)} custom-call(f32[1,8,16,8,128]{4,3,2,1,0:T(8,128)S(1)} %broadcast_in_dim.12.list_ref, s32[16,8,8,128]{3,2,1,0:T(8,128)S(1)} %bitcast.14, f32[16,8,8,128]{3,2,1,0:T(8,128)S(1)} %bitcast.15, f32[16,8,8,128]{3,2,1,0:T(8,128)S(1)} %bitcast.16, f32[3,8,16,8,128]{4,3,2,1,0:T(8,128)S(1)} %bitcast.10, ...), custom_call_target="tpu_custom_call" | custom-call | tf_op jit(solution)/shard_map/binning/pallas_call | solution.py:539
  74.1 1.1 %copy.15 = f32[5,16,32,128]{3,2,1,0:T(8,128)} copy(f32[5,16,32,128]{3,2,1,0:T(8,128)S(1)} %bitcast.13) | data formatting | bytes 2621440
  (2 shorter events, 0.0 us)
Async XLA Ops:
  3.1 1.3 %copy-start = (f32[5,16,32,128]{3,2,1,0:T(8,128)S(1)}, f32[5,16,32,128]{3,2,1,0:T(8,128)}, u32[]{:S(2)}) copy-start(f32[5,16,32,128]{3,2,1,0:T(8,128)} %param.10) | copy-start | bytes 3932164
  4.4 0.9 %copy-start.4 = (f32[16,32,128]{2,1,0:T(8,128)S(1)}, f32[16,32,128]{2,1,0:T(8,128)}, u32[]{:S(2)}) copy-start(f32[16,32,128]{2,1,0:T(8,128)} %param.11) | copy-start | bytes 786436
  5.3 0.7 copy-start.5
  63.9 1.0 %copy-start.1 = (s32[1,128,4,2,128]{4,3,2,1,0:T(2,128)S(1)}, s32[1,128,4,2,128]{4,3,2,1,0:T(2,128)}, u32[]{:S(2)}) copy-start(s32[1,128,4,2,128]{4,3,2,1,0:T(2,128)} %param.17) | copy-start | bytes 1572868
  64.9 1.0 %copy-start.2 = (f32[1,128,4,2,128]{4,3,2,1,0:T(2,128)S(1)}, f32[1,128,4,2,128]{4,3,2,1,0:T(2,128)}, u32[]{:S(2)}) copy-start(f32[1,128,4,2,128]{4,3,2,1,0:T(2,128)} %param.18) | copy-start | bytes 1572868
  66.0 1.0 %copy-start.3 = (f32[1,128,4,2,128]{4,3,2,1,0:T(2,128)S(1)}, f32[1,128,4,2,128]{4,3,2,1,0:T(2,128)}, u32[]{:S(2)}) copy-start(f32[1,128,4,2,128]{4,3,2,1,0:T(2,128)} %param.19) | copy-start | bytes 1572868

commit v2 on v1

--- a/solution.py
+++ b/solution.py
@@ -1,3 +1,5 @@
+import functools
+
 import jax
 import jax.numpy as jnp
 from jax import lax
@@ -27,14 +29,26 @@
 
 
 def step_kernel(
-    x_ref,
+    free,
+    x_hbm,
+    damp_hbm,
+    jac_hbm,
+    fw_hbm,
+    shift_hbm,
+    list_hbm,
+    count_hbm,
+    new_ref,
+    lists_ref,
+    early_ref,
+    middle_ref,
+    late_ref,
     damp_ref,
     jac_ref,
     fw_ref,
     shift_ref,
     list_ref,
-    new_ref,
-    gather_ref,
+    count_ref,
+    weight,
     s1,
     s2,
     s3,
@@ -45,16 +59,18 @@
     ghost_hi,
     row_out,
     row_sel,
-    held1,
-    held2,
-    held3,
-    held4,
-    in1,
-    in2,
-    in3,
-    in4,
+    held,
+    incoming,
+    near1,
+    near2,
+    near3,
     window,
-    parcel,
+    list_out,
+    list_mid,
+    list_stage,
+    parcel0,
+    parcel1,
+    parcel2,
     load_sem,
     theta_send,
     theta_recv,
@@ -64,10 +80,14 @@
     row_recv,
     sel_send,
     sel_recv,
+    list_send,
+    list_recv,
     ring_send,
     ring_recv,
     line_send,
     line_recv,
+    pair_send,
+    pair_recv,
 ):
     a = lax.axis_index("sector")
     b = lax.axis_index("axial")
@@ -78,11 +98,27 @@
     has_lo = jnp.logical_and(b > 0, jnp.logical_not(aft))
     has_hi = jnp.logical_and(b < NB - 1, jnp.logical_not(front))
     states = [s1, s2, s3, s4]
-    row_held = [held1, held2, held3, held4]
-    row_in = [in1, in2, in3, in4]
-
-    load = pltpu.make_async_copy(x_ref, s1.at[:, pl.ds(CZ, ROWS), :], load_sem.at[0])
-    load.start()
+    direct = [k for k in range(4) if k != free]
+    near = dict(zip(direct, (near1, near2, near3)))
+    parcels = [parcel0, parcel1, parcel2]
+    gathers = [early_ref, middle_ref, late_ref]
+
+    loads = [
+        pltpu.make_async_copy(source, target, load_sem.at[n])
+        for n, (source, target) in enumerate(
+            (
+                (x_hbm, s1.at[:, pl.ds(CZ, ROWS), :]),
+                (fw_hbm, fw_ref),
+                (list_hbm, list_ref),
+                (count_hbm, count_ref),
+                (shift_hbm, shift_ref),
+                (jac_hbm, jac_ref),
+                (damp_hbm, damp_ref),
+            )
+        )
+    ]
+    for load in loads:
+        load.start()
 
     barrier = pltpu.get_barrier_semaphore()
 
@@ -100,8 +136,8 @@
         def _(step):
             pl.semaphore_signal(barrier, inc=1, device_id=(step, other), device_id_type=MESH)
 
-    row_out[...] = jnp.zeros_like(row_out)
-    parcel[...] = jnp.zeros_like(parcel)
+    window[...] = jnp.zeros_like(window)
+    weight[...] = jnp.zeros_like(weight)
     for k in range(4):
         @pl.when(b == 0)
         def _():
@@ -111,40 +147,92 @@
         def _():
             ghost_hi[k] = jnp.zeros((NV, CT, NR), jnp.float32)
 
-    pl.semaphore_wait(barrier, jnp.where(interface, NA - 1 + NB - 1 + NA, NA - 1 + NB - 1))
-
-    def ring_start(which):
-        slot = pl.multiple_of((b * NA + a) * PIECE, PIECE)
-        gather_ref[which, pl.ds(slot, PIECE), :] = parcel[which]
+
+    def list_rows(n):
+        return pl.ds(pl.multiple_of(n * NB, NB), NB)
+
+    def list_first():
+        list_mid[list_rows(a), :] = list_out[list_rows(a), :]
 
         @pl.loop(1, NA)
         def _(step):
+            to = lax.rem(a + step, NA)
             pltpu.make_async_remote_copy(
-                src_ref=parcel.at[which],
-                dst_ref=gather_ref.at[which, pl.ds(slot, PIECE), :],
+                src_ref=list_out.at[list_rows(to), :],
+                dst_ref=list_mid.at[list_rows(a), :],
+                send_sem=list_send.at[0],
+                recv_sem=list_recv.at[0],
+                device_id=(to, b),
+                device_id_type=MESH,
+            ).start()
+
+    def list_second():
+        wait_rows(list_mid.at[pl.ds(0, (NA - 1) * NB), :], list_recv.at[0])
+        for n in range(NB):
+            list_stage[n] = list_mid[pl.ds(n, NA, stride=NB), :]
+        lists_ref[b] = list_stage[b]
+
+        @pl.loop(1, NB)
+        def _(step):
+            to = lax.rem(b + step, NB)
+            pltpu.make_async_remote_copy(
+                src_ref=list_stage.at[to],
+                dst_ref=lists_ref.at[b],
+                send_sem=list_send.at[1],
+                recv_sem=list_recv.at[1],
+                device_id=(a, to),
+                device_id_type=MESH,
+            ).start()
+
+    def list_wait():
+        wait_rows(lists_ref.at[pl.ds(0, NB - 1)], list_recv.at[1])
+        wait_rows(list_mid.at[pl.ds(0, (NA - 1) * NB), :], list_send.at[0])
+        wait_rows(lists_ref.at[pl.ds(0, NB - 1)], list_send.at[1])
+
+    core = lax.rem(a, 2)
+    chip = a // 2
+
+    def ring_start(which):
+        gathers[which][b, core, chip] = parcels[which][...]
+
+        @pl.loop(1, NA // 2)
+        def _(step):
+            pltpu.make_async_remote_copy(
+                src_ref=parcels[which],
+                dst_ref=gathers[which].at[b, core, chip],
                 send_sem=ring_send.at[which],
                 recv_sem=ring_recv.at[which],
-                device_id=(lax.rem(a + step, NA), b),
+                device_id=(lax.rem(a + 2 * step, NA), b),
                 device_id_type=MESH,
             ).start()
 
     def line_start(which):
-        wait_rows(gather_ref.at[which, pl.ds(0, (NA - 1) * PIECE), :], ring_recv.at[which])
-        slot = pl.multiple_of(b * NA * PIECE, NA * PIECE)
+        wait_rows(gathers[which].at[0, 0, pl.ds(0, NA // 2 - 1)], ring_recv.at[which])
 
         @pl.loop(1, NB)
         def _(step):
             pltpu.make_async_remote_copy(
-                src_ref=gather_ref.at[which, pl.ds(slot, NA * PIECE), :],
-                dst_ref=gather_ref.at[which, pl.ds(slot, NA * PIECE), :],
+                src_ref=gathers[which].at[b, core],
+                dst_ref=gathers[which].at[b, core],
                 send_sem=line_send.at[which],
                 recv_sem=line_recv.at[which],
                 device_id=(a, lax.rem(b + step, NB)),
                 device_id_type=MESH,
             ).start()
 
-    def line_wait(which):
-        wait_rows(gather_ref.at[which, pl.ds(0, (NB - 1) * NA * PIECE), :], line_recv.at[which])
+    def pair_copy(which):
+        return pltpu.make_async_remote_copy(
+            src_ref=gathers[which].at[:, core],
+            dst_ref=gathers[which].at[:, core],
+            send_sem=pair_send.at[which],
+            recv_sem=pair_recv.at[which],
+            device_id=(a + 1 - 2 * core, b),
+            device_id_type=MESH,
+        )
+
+    def pair_start(which):
+        wait_rows(gathers[which].at[pl.ds(0, NB - 1), 0], line_recv.at[which])
+        pair_copy(which).start()
 
     def theta_copies(k):
         state = states[k]
@@ -191,25 +279,44 @@
         @pl.when(front)
         def _():
             for v in range(NV):
-                row_out[k, pl.ds(v, CT, stride=PIECE), :] = state[v, pl.ds(CZ + CZ - 1, CT, stride=CZ), :]
+                window[pl.ds(v, CT, stride=PIECE), :] = state[v, pl.ds(CZ + CZ - 1, CT, stride=CZ), :]
 
         @pl.when(aft)
         def _():
             for v in range(NV):
-                row_out[k, pl.ds(v, CT, stride=PIECE), :] = state[v, pl.ds(CZ, CT, stride=CZ), :]
+                window[pl.ds(v, CT, stride=PIECE), :] = state[v, pl.ds(CZ, CT, stride=CZ), :]
 
         @pl.when(interface)
         def _():
-            @pl.loop(0, CT)
-            def _(t):
-                pltpu.make_async_remote_copy(
-                    src_ref=row_out.at[k, pl.ds(pl.multiple_of(t * PIECE, PIECE), PIECE), :],
-                    dst_ref=row_held[k].at[a],
-                    send_sem=row_send.at[k],
-                    recv_sem=row_recv.at[k],
-                    device_id=(t, other),
-                    device_id_type=MESH,
-                ).start()
+            for t in range(CT):
+                row_out[k, t] = window[pl.ds(t * PIECE, PIECE), :]
+
+            if k == free:
+                @pl.loop(0, CT)
+                def _(t):
+                    pltpu.make_async_remote_copy(
+                        src_ref=row_out.at[k, t],
+                        dst_ref=held.at[a],
+                        send_sem=row_send.at[k],
+                        recv_sem=row_recv.at[k],
+                        device_id=(t, other),
+                        device_id_type=MESH,
+                    ).start()
+            else:
+                for target, first, place, count in (
+                    (a, 0, 8, 16),
+                    (a + 8, 0, jnp.where(front, 48, 32), 16),
+                    (a + jnp.where(front, 9, 7), 0, jnp.where(front, 32, 48), 16),
+                    (a + jnp.where(front, NA - 1, 1), jnp.where(front, 0, 8), jnp.where(front, 24, 0), 8),
+                ):
+                    pltpu.make_async_remote_copy(
+                        src_ref=row_out.at[k, pl.ds(first, count), pl.ds(0, NV), :],
+                        dst_ref=near[k].at[pl.ds(place, count), pl.ds(0, NV), :],
+                        send_sem=row_send.at[k],
+                        recv_sem=row_recv.at[k],
+                        device_id=(lax.rem(target, NA), other),
+                        device_id_type=MESH,
+                    ).start()
 
         down, up = theta_copies(k)
         down.start()
@@ -232,36 +339,45 @@
         r = shift_ref[k]
         return jnp.where(front, r, (CT * NA - r) & (CT * NA - 1))
 
-    def relay(k):
+    def relay():
         @pl.when(interface)
         def _():
-            wait_rows(row_held[k], row_recv.at[k])
-            first = (turn(k) - a + CT - 1) >> 4
+            wait_rows(held, row_recv.at[free])
+            first = (turn(free) - a + CT - 1) >> 4
 
             @pl.loop(0, NA)
             def _(d):
-                row_sel[k, d] = row_held[k][(d + first) & (NA - 1)]
+                row_sel[d] = held[(d + first) & (NA - 1)]
 
             @pl.loop(1, NA)
             def _(step):
                 d = lax.rem(a + step, NA)
                 pltpu.make_async_remote_copy(
-                    src_ref=row_sel.at[k, d],
-                    dst_ref=row_in[k].at[a],
-                    send_sem=sel_send.at[k],
-                    recv_sem=sel_recv.at[k],
+                    src_ref=row_sel.at[d],
+                    dst_ref=incoming.at[a],
+                    send_sem=sel_send.at[0],
+                    recv_sem=sel_recv.at[0],
                     device_id=(d, b),
                     device_id_type=MESH,
                 ).start()
-            row_in[k][a] = row_sel[k, a]
+            incoming[a] = row_sel[a]
 
     def land(k):
         @pl.when(interface)
         def _():
-            wait_rows(row_in[k].at[pl.ds(0, NA - 1)], sel_recv.at[k])
-            r = turn(k)
-            for t in range(CT):
-                window[pl.ds(t * PIECE, PIECE), :] = row_in[k][(r + t) & (CT - 1)]
+            if k == free:
+                wait_rows(incoming.at[pl.ds(0, NA - 1)], sel_recv.at[0])
+                r = turn(k)
+                for t in range(CT):
+                    window[pl.ds(t * PIECE, PIECE), :] = incoming[(r + t) & (CT - 1)]
+            else:
+                wait_rows(near[k].at[pl.ds(0, 56), pl.ds(0, NV), :], row_recv.at[k])
+                r = shift_ref[k]
+                ahead = jnp.where(r == 0, 8, jnp.where(r == 255, 7, r - 96))
+                behind = jnp.where(r == 0, 8, jnp.where(r == 255, 9, 176 - r))
+                first = jnp.where(front, ahead, behind)
+                for t in range(CT):
+                    window[pl.ds(t * PIECE, PIECE), :] = near[k][(first + t) & 63]
 
         @pl.when(front)
         def _():
@@ -309,7 +425,7 @@
                 total[j] = both if d == 0 else total[j] + both
                 slope = upper - lower
                 for i in range(NV):
-                    term = (0.5 * jac_ref[d, i, j]) * slope
+                    term = (0.5 * jac_ref[i, d, j]) * slope
                     advection[i] = term if advection[i] is None else advection[i] + term
         drag = damp_ref[pl.ds(base, CZ), :] + 6.0 * viscosity
         for i in range(NV):
@@ -330,7 +446,7 @@
             for i in range(NV):
                 rate = viscosity * values[i]
                 for j in range(NV):
-                    rate = rate + (sign * jac_ref[1, i, j]) * values[j]
+                    rate = rate + (sign * jac_ref[i, 1, j]) * values[j]
                 if k < 3:
                     scale = time_step if k == 2 else 0.5 * time_step
                     where = pl.ds(CZ + row, CT, stride=CZ)
@@ -352,38 +468,49 @@
                 precision=lax.Precision.HIGHEST,
                 preferred_element_type=jnp.float32,
             )
-            term = column[0:1] * fw_ref[v]
+            term = column[0:1] * weight[v : v + 1, :]
             total = term if total is None else total + term
         for block in range(4):
-            row = 2 * block + k % 2
-            parcel[1 + k // 2, row : row + 1, :] = total[:, block * 128 : (block + 1) * 128]
-
-    parcel[0] = list_ref[...]
-    ring_start(0)
-    load.wait()
+            part = total[:, block * 128 : (block + 1) * 128]
+            if k == 3:
+                parcel2[block : block + 1, :] = part
+            elif k == 2:
+                parcel1[block : block + 1, :] = part
+            else:
+                parcel0[2 * block + k : 2 * block + k + 1, :] = part
+
+    for load in loads:
+        load.wait()
+    for t in range(CT):
+        weight[0:NV, t * CZ : (t + 1) * CZ] = fw_ref[:, t, :]
+    rows = jnp.concatenate([list_ref[...], count_ref[...], jnp.zeros((3, NR), jnp.int32)], 0).astype(jnp.float32)
+    places = lax.broadcasted_iota(jnp.int32, (8, NR), 0) == lax.broadcasted_iota(jnp.int32, (8, NR), 1)
+    list_out[...] = lax.dot_general(
+        rows,
+        places.astype(jnp.float32),
+        (((0,), (0,)), ((), ())),
+        precision=lax.Precision.HIGHEST,
+        preferred_element_type=jnp.float32,
+    )
+    sample(0)
+    pl.semaphore_wait(barrier, jnp.where(interface, NA - 1 + NB - 1 + NA, NA - 1 + NB - 1))
     send_edges(0)
+    list_first()
     for k in range(4):
         @pl.loop(1, CT // 2)
         def _(t):
             plane(k, t)
 
-        relay(k)
+        if k == free:
+            relay()
 
         @pl.loop(CT // 2, CT - 1)
         def _(t):
             plane(k, t)
 
-        if k == 0:
-            sample(0)
-            line_start(0)
-        elif k == 1:
-            sample(1)
-            ring_start(1)
-        elif k == 2:
-            line_start(1)
-            sample(2)
-        else:
+        if k == 3:
             line_start(2)
+            pair_start(1)
         down, up = theta_copies(k)
         down.wait_recv()
         up.wait_recv()
@@ -396,14 +523,26 @@
         correct(k)
         if k < 3:
             send_edges(k + 1)
-        if k == 2:
+        if k == 0:
+            sample(1)
+            ring_start(0)
+            list_second()
+        elif k == 1:
+            sample(2)
+            ring_start(1)
+            line_start(0)
+        elif k == 2:
             sample(3)
             ring_start(2)
-
+            line_start(1)
+            pair_start(0)
+
+    pair_start(2)
+    list_wait()
     for which in range(3):
-        line_wait(which)
-        wait_rows(gather_ref.at[which, pl.ds(0, (NA - 1) * PIECE), :], ring_send.at[which])
-        wait_rows(gather_ref.at[which, pl.ds(0, (NB - 1) * NA * PIECE), :], line_send.at[which])
+        wait_rows(gathers[which].at[0, 0, pl.ds(0, NA // 2 - 1)], ring_send.at[which])
+        wait_rows(gathers[which].at[pl.ds(0, NB - 1), 0], line_send.at[which])
+        pair_copy(which).wait()
     for k in range(4):
         down, up = theta_copies(k)
         down.wait_send()
@@ -420,43 +559,64 @@
 
         @pl.when(interface)
         def _():
-            wait_rows(row_out.at[k], row_send.at[k])
-            wait_rows(row_sel.at[k, pl.ds(0, NA - 1)], sel_send.at[k])
-
-
-def step_call(x, damping, jacobians, face_weight, phase_shift, lists):
+            if k == free:
+                wait_rows(row_out.at[k], row_send.at[k])
+                wait_rows(row_sel.at[pl.ds(0, NA - 1)], sel_send.at[0])
+            else:
+                wait_rows(near[k].at[pl.ds(0, 56), pl.ds(0, NV), :], row_send.at[k])
+
+
+def step_call(free, x, damping, jacobians, face_weight, phase_shift, lists, counts):
     vmem = pl.BlockSpec(memory_space=pltpu.VMEM)
-    smem = pl.BlockSpec(memory_space=pltpu.SMEM)
+    hbm = pl.BlockSpec(memory_space=pltpu.HBM)
     state = pltpu.VMEM((NV, PAD, NR), jnp.float32)
     edge = pltpu.VMEM((4, NV, CT, NR), jnp.float32)
-    row = pltpu.VMEM((4, CT * PIECE, NR), jnp.float32)
-    held = pltpu.VMEM((NA, PIECE, NR), jnp.float32)
+    row = pltpu.VMEM((NA, PIECE, NR), jnp.float32)
     dma = pltpu.SemaphoreType.DMA
     return pl.pallas_call(
-        step_kernel,
+        functools.partial(step_kernel, free),
         out_shape=(
             jax.ShapeDtypeStruct((NV, ROWS, NR), jnp.float32),
-            jax.ShapeDtypeStruct((3, NA * NB * PIECE, NR), jnp.float32),
+            jax.ShapeDtypeStruct((NB, NA, NR), jnp.float32),
+            jax.ShapeDtypeStruct((NB, 2, NA // 2, 8, NR), jnp.float32),
+            jax.ShapeDtypeStruct((NB, 2, NA // 2, 4, NR), jnp.float32),
+            jax.ShapeDtypeStruct((NB, 2, NA // 2, 4, NR), jnp.float32),
         ),
-        in_specs=[pl.BlockSpec(memory_space=pl.ANY), vmem, smem, vmem, smem, vmem],
-        out_specs=(vmem, vmem),
-        scratch_shapes=[state] * 4
+        in_specs=[hbm] * 7,
+        out_specs=(vmem,) * 5,
+        scratch_shapes=[
+            pltpu.VMEM((ROWS, NR), jnp.float32),
+            pltpu.SMEM((NV, 3, NV), jnp.float32),
+            pltpu.VMEM((NV, CT, CZ), jnp.float32),
+            pltpu.SMEM((4,), jnp.int32),
+            pltpu.VMEM((4, NR), jnp.int32),
+            pltpu.VMEM((1, NR), jnp.int32),
+            pltpu.VMEM((8, ROWS), jnp.float32),
+        ]
+        + [state] * 4
         + [edge] * 4
-        + [row, pltpu.VMEM((4, NA, PIECE, NR), jnp.float32)]
-        + [held] * 8
-        + [pltpu.VMEM((CT * PIECE, NR), jnp.float32), pltpu.VMEM((3, PIECE, NR), jnp.float32)]
-        + [dma((1,)), dma((4, 2)), dma((4, 2)), dma((4, 2)), dma((4, 2))]
-        + [dma((4,))] * 4
-        + [dma((3,))] * 4,
+        + [pltpu.VMEM((4, CT, PIECE, NR), jnp.float32), row, row, row]
+        + [pltpu.VMEM((64, PIECE, NR), jnp.float32)] * 3
+        + [pltpu.VMEM((CT * PIECE, NR), jnp.float32)]
+        + [pltpu.VMEM((NA * NB, NR), jnp.float32)] * 2
+        + [pltpu.VMEM((NB, NA, NR), jnp.float32)]
+        + [pltpu.VMEM((rows, NR), jnp.float32) for rows in (8, 4, 4)]
+        + [dma((7,)), dma((4, 2)), dma((4, 2)), dma((4, 2)), dma((4, 2))]
+        + [dma((4,)), dma((4,)), dma((1,)), dma((1,))]
+        + [dma((2,))] * 2
+        + [dma((3,))] * 6,
         compiler_params=pltpu.CompilerParams(
-            collective_id=0, has_side_effects=True, vmem_limit_bytes=40 << 20
+            collective_id=free, has_side_effects=True, vmem_limit_bytes=24 << 20
         ),
-        name="substeps",
-    )(x, damping, jacobians, face_weight, phase_shift, lists)
-
-
-def bin_kernel(list_ref, bin_ref, fraction_ref, gain_ref, early_ref, late_ref, out_ref, total):
+        name="substeps%d" % free,
+    )(x, damping, jacobians, face_weight, phase_shift, lists, counts)
+
+
+def bin_kernel(
+    list_ref, bin_ref, fraction_ref, gain_ref, early_ref, middle_ref, late_ref, state_ref, out_ref, new_ref, total
+):
     step = pl.program_id(0)
+    new_ref[...] = state_ref[...]
 
     @pl.when(step == 0)
     def _():
@@ -473,25 +633,36 @@
     def spread(ref, row):
         return jnp.broadcast_to(ref[row : row + 1], (8, 128))
 
+    spot = lax.broadcasted_iota(jnp.int32, (128, 5 * 128), 0)
+    part_of = lax.broadcasted_iota(jnp.int32, (128, 5 * 128), 1) // 128
+    wide = jnp.dot(
+        list_ref[0].astype(jnp.bfloat16),
+        (spot == part_of).astype(jnp.bfloat16),
+        preferred_element_type=jnp.float32,
+    )
+
+    def entry(a, c):
+        return jnp.broadcast_to(wide[a : a + 1, c * 128 : (c + 1) * 128], (8, 128))
+
     for a in range(NA):
         gain = gain_ref[a, 0]
         fraction = fraction_ref[a, 0]
         bins = bin_ref[a, 0]
         coarse_bin = (bins >> 5).astype(jnp.float32)
         fine_bin = (bins & 31).astype(jnp.float32)
-        early = early_ref[0, 0, a]
-        late = late_ref[0, 0, a]
-        lists = list_ref[0, 0, a]
+        early = early_ref[0, a % 2, a // 2]
+        middle = middle_ref[0, a % 2, a // 2]
+        late = late_ref[0, a % 2, a // 2]
         blocks = []
         for block in range(4):
-            later = jnp.where(sample == 2, spread(late, 2 * block), spread(late, 2 * block + 1))
+            later = jnp.where(sample == 2, spread(middle, block), spread(late, block))
             later = jnp.where(sample == 1, spread(early, 2 * block + 1), later)
             blocks.append(jnp.where(sample == 0, spread(early, 2 * block), later))
-        count = spread(lists, 4)
+        count = entry(a, 4)
         weights = [[], []]
         selectors = [[], []]
         for c in range(4):
-            listed = spread(lists, c)
+            listed = entry(a, c)
             received = jnp.zeros((8, 128), jnp.float32)
             for block in range(4):
                 received = jnp.where(listed == block, blocks[block], received)
@@ -530,22 +701,35 @@
             out_ref[o : o + 1, :] = signal
 
 
-def bin_call(gathered, lists, bins, fractions, gains):
+def bin_call(lists, bins, fractions, gains, early, middle, late, state):
     owned = pl.BlockSpec((NA, 1, PIECE, 128), lambda s: (0, s, 0, 0))
 
-    def part(which):
-        return pl.BlockSpec((1, 1, NA, PIECE, 128), lambda s: (which, s, 0, 0, 0))
-
+    def part(rows):
+        return pl.BlockSpec((1, 2, NA // 2, rows, 128), lambda s: (s, 0, 0, 0, 0))
+
+    slab = pl.BlockSpec((NV, ROWS // NB, NR), lambda s: (0, s, 0))
     return pl.pallas_call(
         bin_kernel,
         grid=(NB,),
-        in_specs=[part(0), owned, owned, owned, part(1), part(2)],
-        out_specs=pl.BlockSpec((2, NBIN), lambda s: (0, 0)),
-        out_shape=jax.ShapeDtypeStruct((2, NBIN), jnp.float32),
+        in_specs=[
+            pl.BlockSpec((1, NA, 128), lambda s: (s, 0, 0)),
+            owned,
+            owned,
+            owned,
+            part(8),
+            part(4),
+            part(4),
+            slab,
+        ],
+        out_specs=(pl.BlockSpec((2, NBIN), lambda s: (0, 0)), slab),
+        out_shape=(
+            jax.ShapeDtypeStruct((2, NBIN), jnp.float32),
+            jax.ShapeDtypeStruct((NV, ROWS, NR), jnp.float32),
+        ),
         scratch_shapes=[pltpu.VMEM((2, 64, 32), jnp.float32)],
-        compiler_params=pltpu.CompilerParams(vmem_limit_bytes=40 << 20),
+        compiler_params=pltpu.CompilerParams(vmem_limit_bytes=24 << 20),
         name="binning",
-    )(lists, bins, fractions, gains, gathered, gathered)
+    )(lists, bins, fractions, gains, early, middle, late, state)
 
 
 def local(
@@ -560,26 +744,36 @@
     arrival_fraction,
     arrival_gain,
 ):
-    lists = jnp.concatenate(
-        [face_list[0].T, face_count, jnp.zeros((3, NA * NB), jnp.int32)], axis=0
-    ).astype(jnp.float32)
-    new_state, gathered = step_call(
+    zero = phase_shift == 0
+    last = phase_shift == CT * NA - 1
+    opposite = jnp.logical_and(phase_shift >= 128, phase_shift < 144)
+    apart = jnp.logical_not(jnp.eye(4, dtype=bool))
+
+    def elsewhere(flags):
+        return jnp.any(jnp.logical_and(apart, flags[None, :]), axis=1)
+
+    rest = elsewhere(zero) & elsewhere(last) & elsewhere(opposite)
+    free = jnp.min(jnp.where(rest, jnp.arange(4, dtype=jnp.int32), 3))
+    state, lists, early, middle, late = lax.switch(
+        free,
+        [functools.partial(step_call, k) for k in range(4)],
         flow_state.reshape(NV, ROWS, NR),
         damping.reshape(ROWS, NR),
-        jacobians,
-        face_weight.reshape(NV, 1, ROWS),
+        jnp.transpose(jacobians, (1, 0, 2)),
+        face_weight,
         phase_shift,
-        lists,
+        face_list[0].T,
+        face_count,
     )
-    owner = lax.axis_index("sector") * NB + lax.axis_index("axial")
-    mine = lax.dynamic_slice_in_dim(gathered[0], owner, 1, axis=1)
-    lists = jnp.broadcast_to(mine, (NA * NB * PIECE, NR)).reshape(1, NB, NA, PIECE, NR)
-    signal = bin_call(
-        gathered.reshape(3, NB, NA, PIECE, NR),
+    signal, new_state = bin_call(
         lists,
         arrival_bin.reshape(NA, NB, PIECE, 128),
         arrival_fraction.reshape(NA, NB, PIECE, 128),
         arrival_gain.reshape(NA, NB, PIECE, 128),
+        early,
+        middle,
+        late,
+        state,
     )
     return new_state.reshape(NV, CT, CZ, NR), signal
 

time: 75.7 us -> 57 us (0.75)
  Pallas kernels: 65 us -> 53.3 us
  local copies, waits for them, and re-layouts: 8.71 us -> 0.02 us
  other arithmetic: 0.77 us -> 1.58 us
    pallas_call x2, Pallas kernels: 65 us -> 53.3 us  [the longest x1 44.1 us: step_call(): pl.pallas_call(functools.partial(step_kernel, free), out_shape=(jax.Shape...]
    unnamed x14 -> x6, local copies, waits for them, and re-layouts: 7.09 us -> 0.02 us
    reshape x1 -> x0, local copies, waits for them, and re-layouts: 0.86 us -> none  [local(): face_weight.reshape(NV, 1, ROWS)]
    convert_element_type x1 -> x0, other arithmetic: 0.77 us -> none  [local(): lists = jnp.concatenate([face_list[0].T, face_count, jnp.zeros((3, NA * N...]
where the time goes in v2:
time: 57 us; the launch traced here: 56.8 us
  Pallas kernels  53.3 us (94%)
  other arithmetic  1.58 us (3%)
  between operations  1.34 us (2%)
    pallas_call x1, Pallas kernels, step_call(): pl.pallas_call(functools.partial(step_kernel, free), out_shape=(jax.Shape...  44.1 us
    pallas_call x1, Pallas kernels, bin_call(): pl.pallas_call(bin_kernel, grid=(NB,), in_specs=[pl.BlockSpec((1, NA, 128...  9.22 us

profile of v2, /device:TPU:1, one launch (start us, length us, event | category | flops | bytes accessed | tf_op | source)
XLA Modules:
  0.0 56.8 jit_solution(18081232481172614439)
XLA Ops:
  0.6 0.7 %broadcast_compare_fusion = (pred[4]{0:T(512)(128)(4,1)S(1)}, pred[4]{0:T(512)(128)(4,1)S(1)}, pred[4]{0:T(512)(128)(4,1)S(1)}) fusion(s32[4]{0:T(128)} %param.18), kind=kLoop, calls=%fused_computation.11 | loop fusion | flops 20 | bytes 28 | tf_op jit(solution)/shard_map/eq | solution.py:748
  1.3 0.1 fusion.4
  1.4 0.1 fusion.6
  1.6 0.6 %fusion.7 = s32[]{:T(128)} fusion(pred[4]{0:T(512)(128)(4,1)S(1)} %fusion.6, pred[4]{0:T(512)(128)(4,1)S(1)} %get-tuple-element.103, pred[4]{0:T(512)(128)(4,1)S(1)} %get-tuple-element.104), kind=kLoop, calls=%fused_computation.10 | loop fusion | flops 15 | bytes 16 | tf_op jit(solution)/shard_map/reduce_min | solution.py:756
  2.9 0.0 copy-start
  2.9 0.0 copy-start.1
  2.9 0.0 copy-start.2
  2.9 44.7 %conditional.1 = ((f32[5,512,128]{2,1,0:T(8,128)S(1)}, f32[8,16,128]{2,1,0:T(8,128)S(1)}, f32[8,2,8,8,128]{4,3,2,1,0:T(8,128)S(1)}, f32[8,2,8,4,128]{4,3,2,1,0:T(4,128)}, f32[8,2,8,4,128]{4,3,2,1,0:T(4,128)})) conditional(s32[]{:T(128)} %clamp.3, (f32[5,512,128]{2,1,0:T(8,128)}, f32[512,128]{1,0:T(8,128)}, ...), branch_computations={%region_4.5_spmd, %region_5.6_spmd, %region_6.7_spmd, %region_7.8_... | conditional | bytes 8 | solution.py:757
  3.1 44.1 %substeps2.1 = (f32[5,512,128]{2,1,0:T(8,128)S(1)}, f32[8,16,128]{2,1,0:T(8,128)S(1)}, f32[8,2,8,8,128]{4,3,2,1,0:T(8,128)S(1)}, f32[8,2,8,4,128]{4,3,2,1,0:T(4,128)}, f32[8,2,8,4,128]{4,3,2,1,0:T(4,128)}) custom-call(f32[5,512,128]{2,1,0:T(8,128)} %get-tuple-element.70.x_hbm, f32[512,128]{1,0:T(8,128)} %get-tuple-element.71.damp_hbm, ...), custom_call_target="tpu_custom_call" | custom-call | tf_op jit(solution)/shard_map/cond/branch_2_fun/substeps2/pallas_call | solution.py:576
  47.6 0.0 copy-done
  47.6 0.0 copy-done.1
  47.6 0.0 copy-done.2
  47.6 9.2 %binning.1 = (f32[2,128]{1,0:T(2,128)}, f32[5,512,128]{2,1,0:T(8,128)}) custom-call(f32[8,16,128]{2,1,0:T(8,128)S(1)} %get-tuple-element.93.list_ref, s32[16,8,8,128]{3,2,1,0:T(8,128)S(1)} %bitcast.10, f32[16,8,8,128]{3,2,1,0:T(8,128)S(1)} %bitcast.11, f32[16,8,8,128]{3,2,1,0:T(8,128)S(1)} %bitcast.12, f32[8,2,8,8,128]{4,3,2,1,0:T(8,128)S(1)} %get-tuple-element.94.early_ref, ...), custom_call_target="tpu_custom_call" | custom-call | tf_op jit(solution)/shard_map/binning/pallas_call | solution.py:711
Async XLA Ops:
  2.9 44.7 %copy-start = (s32[1,128,4,2,128]{4,3,2,1,0:T(2,128)S(1)}, s32[1,128,4,2,128]{4,3,2,1,0:T(2,128)}, u32[]{:S(2)}) copy-start(s32[1,128,4,2,128]{4,3,2,1,0:T(2,128)} %param.21) | copy-start | bytes 1572868
  2.9 44.7 %copy-start.1 = (f32[1,128,4,2,128]{4,3,2,1,0:T(2,128)S(1)}, f32[1,128,4,2,128]{4,3,2,1,0:T(2,128)}, u32[]{:S(2)}) copy-start(f32[1,128,4,2,128]{4,3,2,1,0:T(2,128)} %param.22) | copy-start | bytes 1572868
  2.9 44.7 %copy-start.2 = (f32[1,128,4,2,128]{4,3,2,1,0:T(2,128)S(1)}, f32[1,128,4,2,128]{4,3,2,1,0:T(2,128)}, u32[]{:S(2)}) copy-start(f32[1,128,4,2,128]{4,3,2,1,0:T(2,128)} %param.23) | copy-start | bytes 1572868

commit v3 on v2

--- a/solution.py
+++ b/solution.py
@@ -37,11 +37,22 @@
     shift_hbm,
     list_hbm,
     count_hbm,
+    bin_hbm,
+    fraction_hbm,
+    gain_hbm,
     new_ref,
+    signal_ref,
     lists_ref,
     early_ref,
     middle_ref,
     late_ref,
+    bin_ref,
+    fraction_ref,
+    gain_ref,
+    selector_ref,
+    wide_ref,
+    total,
+    last_total,
     damp_ref,
     jac_ref,
     fw_ref,
@@ -114,6 +125,9 @@
                 (shift_hbm, shift_ref),
                 (jac_hbm, jac_ref),
                 (damp_hbm, damp_ref),
+                (bin_hbm, bin_ref),
+                (fraction_hbm, fraction_ref),
+                (gain_hbm, gain_ref),
             )
         )
     ]
@@ -479,7 +493,129 @@
             else:
                 parcel0[2 * block + k : 2 * block + k + 1, :] = part
 
-    for load in loads:
+    def spread(row):
+        return jnp.broadcast_to(row, (8, 128))
+
+    fine = lax.broadcasted_iota(jnp.int32, (32, 128), 0).astype(jnp.float32).astype(jnp.bfloat16)
+    place = lax.broadcasted_iota(jnp.int32, (8, 128), 0)
+    which_sample = place % 4
+
+    def prepare(n):
+        @pl.loop(0, NA)
+        def _(m):
+            fine_bin = (bin_ref[m, n] & 31).astype(jnp.float32)
+            for o in range(2):
+                columns = []
+                for c in range(4):
+                    row = 2 * c + o
+                    within = jnp.broadcast_to(fine_bin[row : row + 1], (32, 128)).astype(jnp.bfloat16)
+                    columns.append(jnp.where(within == fine, jnp.bfloat16(1), jnp.bfloat16(0)))
+                selector_ref[n, m, o] = jnp.concatenate(columns, 1)
+
+    def widen():
+        spot = lax.broadcasted_iota(jnp.int32, (128, 5 * 128), 0)
+        part_of = lax.broadcasted_iota(jnp.int32, (128, 5 * 128), 1) // 128
+        table = (spot == part_of).astype(jnp.bfloat16)
+        for n in range(NB):
+            wide_ref[n] = jnp.dot(
+                lists_ref[n].astype(jnp.bfloat16), table, preferred_element_type=jnp.float32
+            )
+
+    def chosen(n, m, c, blocks):
+        listed = spread(wide_ref[n, m : m + 1, c * 128 : (c + 1) * 128])
+        count = spread(wide_ref[n, m : m + 1, 4 * 128 : 5 * 128])
+        picked = jnp.zeros((8, 128), jnp.float32)
+        for block in range(4):
+            picked = jnp.where(listed == block, blocks[block], picked)
+        return jnp.where(count > c, picked, 0.0)
+
+    def halves(part):
+        head = part.astype(jnp.bfloat16).astype(jnp.float32)
+        return jnp.concatenate([head, part - head], 0).astype(jnp.bfloat16)
+
+    def against(weights, n, m, o):
+        return lax.dot_general(
+            jnp.concatenate(weights, 1),
+            selector_ref[n, m, o],
+            (((1,), (1,)), ((), ())),
+            preferred_element_type=jnp.float32,
+        )
+
+    def bin_first(n):
+        low = place < 4
+        sign = jnp.where(low, -1.0, 1.0).astype(jnp.float32)
+        shift = jnp.where(low, 1.0, 0.0).astype(jnp.float32)
+        zero = jnp.zeros((16, 128), jnp.bfloat16)
+        sums = [jnp.zeros((64, 32), jnp.float32)] * 2
+        for m in range(NA):
+            gain = gain_ref[m, n]
+            fraction = fraction_ref[m, n]
+            coarse_bin = (bin_ref[m, n] >> 5).astype(jnp.float32)
+            early = early_ref[n, m % 2, m // 2]
+            middle = middle_ref[n, m % 2, m // 2]
+            blocks = []
+            for block in range(4):
+                later = jnp.where(which_sample == 2, spread(middle[block : block + 1]), 0.0)
+                later = jnp.where(which_sample == 1, spread(early[2 * block + 1 : 2 * block + 2]), later)
+                blocks.append(jnp.where(which_sample == 0, spread(early[2 * block : 2 * block + 1]), later))
+            weights = [[], []]
+            for c in range(4):
+                received = chosen(n, m, c, blocks)
+                for o in range(2):
+                    row = slice(2 * c + o, 2 * c + o + 1)
+                    both = halves(received * (spread(gain[row]) * (spread(fraction[row]) * sign + shift)))
+                    coarse = jnp.broadcast_to(coarse_bin[row], (16, 128)).astype(jnp.bfloat16)
+                    weights[o].append(
+                        jnp.concatenate([jnp.where(coarse == jnp.bfloat16(q), both, zero) for q in range(4)], 0)
+                    )
+            for o in range(2):
+                sums[o] = sums[o] + against(weights[o], n, m, o)
+        for o in range(2):
+            total[o] += sums[o]
+
+    def bin_last(n):
+        part = place % 2
+        group = (place // 2).astype(jnp.float32)
+        sign = jnp.where(part == 0, -1.0, 1.0).astype(jnp.float32)
+        shift = jnp.where(part == 0, 1.0, 0.0).astype(jnp.float32)
+        sums = [jnp.zeros((16, 32), jnp.float32)] * 2
+        for m in range(NA):
+            gain = gain_ref[m, n]
+            fraction = fraction_ref[m, n]
+            coarse_bin = (bin_ref[m, n] >> 5).astype(jnp.float32)
+            late = late_ref[n, m % 2, m // 2]
+            blocks = [spread(late[block : block + 1]) for block in range(4)]
+            weights = [[], []]
+            for c in range(4):
+                received = chosen(n, m, c, blocks)
+                for o in range(2):
+                    row = slice(2 * c + o, 2 * c + o + 1)
+                    scale = spread(gain[row]) * (spread(fraction[row]) * sign + shift)
+                    scale = jnp.where(spread(coarse_bin[row]) == group, scale, 0.0)
+                    weights[o].append(halves(received * scale))
+            for o in range(2):
+                sums[o] = sums[o] + against(weights[o], n, m, o)
+        for o in range(2):
+            last_total[o] += sums[o]
+
+    def emit():
+        for o in range(2):
+            signal = jnp.zeros((1, NBIN), jnp.float32)
+            for q in range(8):
+                if q % 4 < 3:
+                    rows = [(16 * g + q, 16 * g + 8 + q) for g in range(4)]
+                    source = total
+                else:
+                    rows = [(2 * g + q // 4, 8 + 2 * g + q // 4) for g in range(4)]
+                    source = last_total
+                whole = jnp.concatenate([source[o, h : h + 1, :] + source[o, l : l + 1, :] for h, l in rows], 1)
+                offset = q % 4 + q // 4
+                signal = signal + (pltpu.roll(whole, offset, 1) if offset else whole)
+            signal_ref[o : o + 1, :] = signal
+
+    total[...] = jnp.zeros_like(total)
+    last_total[...] = jnp.zeros_like(last_total)
+    for load in loads[:7]:
         load.wait()
     for t in range(CT):
         weight[0:NV, t * CZ : (t + 1) * CZ] = fw_ref[:, t, :]
@@ -496,18 +632,18 @@
     pl.semaphore_wait(barrier, jnp.where(interface, NA - 1 + NB - 1 + NA, NA - 1 + NB - 1))
     send_edges(0)
     list_first()
-    for k in range(4):
-        @pl.loop(1, CT // 2)
-        def _(t):
-            plane(k, t)
-
-        if k == free:
-            relay()
-
-        @pl.loop(CT // 2, CT - 1)
-        def _(t):
-            plane(k, t)
-
+    def between(k):
+        if k == 0:
+            for load in loads[7:]:
+                load.wait()
+
+        @pl.loop(2 * k, 2 * k + 2)
+        def _(n):
+            prepare(n)
+
+        if k == 2:
+            list_wait()
+            widen()
         if k == 3:
             line_start(2)
             pair_start(1)
@@ -515,9 +651,19 @@
         down.wait_recv()
         up.wait_recv()
 
-        @pl.loop(0, 2)
-        def _(side):
-            plane(k, side * (CT - 1))
+    for k in range(4):
+        @pl.loop(0, CT)
+        def _(step):
+            if k == free:
+                @pl.when(step == CT // 2)
+                def _():
+                    relay()
+
+            @pl.when(step == CT - 2)
+            def _():
+                between(k)
+
+            plane(k, lax.rem(step + 1, CT))
 
         land(k)
         correct(k)
@@ -537,12 +683,28 @@
             line_start(1)
             pair_start(0)
 
-    pair_start(2)
-    list_wait()
+    for which in range(2):
+        pair_copy(which).wait_recv()
+
+    @pl.loop(0, NB)
+    def _(n):
+        @pl.when(n == NB // 2)
+        def _():
+            pair_start(2)
+
+        bin_first(n)
+
+    pair_copy(2).wait_recv()
+
+    @pl.loop(0, NB)
+    def _(n):
+        bin_last(n)
+
+    emit()
     for which in range(3):
         wait_rows(gathers[which].at[0, 0, pl.ds(0, NA // 2 - 1)], ring_send.at[which])
         wait_rows(gathers[which].at[pl.ds(0, NB - 1), 0], line_send.at[which])
-        pair_copy(which).wait()
+        pair_copy(which).wait_send()
     for k in range(4):
         down, up = theta_copies(k)
         down.wait_send()
@@ -566,7 +728,9 @@
                 wait_rows(near[k].at[pl.ds(0, 56), pl.ds(0, NV), :], row_send.at[k])
 
 
-def step_call(free, x, damping, jacobians, face_weight, phase_shift, lists, counts):
+def step_call(
+    free, x, damping, jacobians, face_weight, phase_shift, lists, counts, bins, fractions, gains
+):
     vmem = pl.BlockSpec(memory_space=pltpu.VMEM)
     hbm = pl.BlockSpec(memory_space=pltpu.HBM)
     state = pltpu.VMEM((NV, PAD, NR), jnp.float32)
@@ -577,14 +741,22 @@
         functools.partial(step_kernel, free),
         out_shape=(
             jax.ShapeDtypeStruct((NV, ROWS, NR), jnp.float32),
-            jax.ShapeDtypeStruct((NB, NA, NR), jnp.float32),
-            jax.ShapeDtypeStruct((NB, 2, NA // 2, 8, NR), jnp.float32),
-            jax.ShapeDtypeStruct((NB, 2, NA // 2, 4, NR), jnp.float32),
-            jax.ShapeDtypeStruct((NB, 2, NA // 2, 4, NR), jnp.float32),
+            jax.ShapeDtypeStruct((2, NBIN), jnp.float32),
         ),
-        in_specs=[hbm] * 7,
-        out_specs=(vmem,) * 5,
+        in_specs=[hbm] * 10,
+        out_specs=(vmem,) * 2,
         scratch_shapes=[
+            pltpu.VMEM((NB, NA, NR), jnp.float32),
+            pltpu.VMEM((NB, 2, NA // 2, 8, NR), jnp.float32),
+            pltpu.VMEM((NB, 2, NA // 2, 4, NR), jnp.float32),
+            pltpu.VMEM((NB, 2, NA // 2, 4, NR), jnp.float32),
+            pltpu.VMEM((NA, NB, PIECE, 128), jnp.int32),
+            pltpu.VMEM((NA, NB, PIECE, 128), jnp.float32),
+            pltpu.VMEM((NA, NB, PIECE, 128), jnp.float32),
+            pltpu.VMEM((NB, NA, 2, 32, 512), jnp.bfloat16),
+            pltpu.VMEM((NB, NA, 5 * 128), jnp.float32),
+            pltpu.VMEM((2, 64, 32), jnp.float32),
+            pltpu.VMEM((2, 16, 32), jnp.float32),
             pltpu.VMEM((ROWS, NR), jnp.float32),
             pltpu.SMEM((NV, 3, NV), jnp.float32),
             pltpu.VMEM((NV, CT, CZ), jnp.float32),
@@ -601,135 +773,15 @@
         + [pltpu.VMEM((NA * NB, NR), jnp.float32)] * 2
         + [pltpu.VMEM((NB, NA, NR), jnp.float32)]
         + [pltpu.VMEM((rows, NR), jnp.float32) for rows in (8, 4, 4)]
-        + [dma((7,)), dma((4, 2)), dma((4, 2)), dma((4, 2)), dma((4, 2))]
+        + [dma((10,)), dma((4, 2)), dma((4, 2)), dma((4, 2)), dma((4, 2))]
         + [dma((4,)), dma((4,)), dma((1,)), dma((1,))]
         + [dma((2,))] * 2
         + [dma((3,))] * 6,
         compiler_params=pltpu.CompilerParams(
-            collective_id=free, has_side_effects=True, vmem_limit_bytes=24 << 20
+            collective_id=free, has_side_effects=True, vmem_limit_bytes=44 << 20
         ),
         name="substeps%d" % free,
-    )(x, damping, jacobians, face_weight, phase_shift, lists, counts)
-
-
-def bin_kernel(
-    list_ref, bin_ref, fraction_ref, gain_ref, early_ref, middle_ref, late_ref, state_ref, out_ref, new_ref, total
-):
-    step = pl.program_id(0)
-    new_ref[...] = state_ref[...]
-
-    @pl.when(step == 0)
-    def _():
-        total[...] = jnp.zeros_like(total)
-
-    place = lax.broadcasted_iota(jnp.int32, (8, 128), 0)
-    low = place < 4
-    sample = place % 4
-    sign = jnp.where(low, -1.0, 1.0).astype(jnp.float32)
-    shift = jnp.where(low, 1.0, 0.0).astype(jnp.float32)
-    fine = lax.broadcasted_iota(jnp.int32, (32, 128), 0).astype(jnp.float32).astype(jnp.bfloat16)
-    zero = jnp.zeros((16, 128), jnp.bfloat16)
-
-    def spread(ref, row):
-        return jnp.broadcast_to(ref[row : row + 1], (8, 128))
-
-    spot = lax.broadcasted_iota(jnp.int32, (128, 5 * 128), 0)
-    part_of = lax.broadcasted_iota(jnp.int32, (128, 5 * 128), 1) // 128
-    wide = jnp.dot(
-        list_ref[0].astype(jnp.bfloat16),
-        (spot == part_of).astype(jnp.bfloat16),
-        preferred_element_type=jnp.float32,
-    )
-
-    def entry(a, c):
-        return jnp.broadcast_to(wide[a : a + 1, c * 128 : (c + 1) * 128], (8, 128))
-
-    for a in range(NA):
-        gain = gain_ref[a, 0]
-        fraction = fraction_ref[a, 0]
-        bins = bin_ref[a, 0]
-        coarse_bin = (bins >> 5).astype(jnp.float32)
-        fine_bin = (bins & 31).astype(jnp.float32)
-        early = early_ref[0, a % 2, a // 2]
-        middle = middle_ref[0, a % 2, a // 2]
-        late = late_ref[0, a % 2, a // 2]
-        blocks = []
-        for block in range(4):
-            later = jnp.where(sample == 2, spread(middle, block), spread(late, block))
-            later = jnp.where(sample == 1, spread(early, 2 * block + 1), later)
-            blocks.append(jnp.where(sample == 0, spread(early, 2 * block), later))
-        count = entry(a, 4)
-        weights = [[], []]
-        selectors = [[], []]
-        for c in range(4):
-            listed = entry(a, c)
-            received = jnp.zeros((8, 128), jnp.float32)
-            for block in range(4):
-                received = jnp.where(listed == block, blocks[block], received)
-            received = jnp.where(count > c, received, 0.0)
-            for o in range(2):
-                row = 2 * c + o
-                part = received * (spread(gain, row) * (spread(fraction, row) * sign + shift))
-                head = part.astype(jnp.bfloat16).astype(jnp.float32)
-                both = jnp.concatenate([head, part - head], 0).astype(jnp.bfloat16)
-                coarse = jnp.broadcast_to(coarse_bin[row : row + 1], (16, 128)).astype(jnp.bfloat16)
-                weights[o].append(
-                    jnp.concatenate([jnp.where(coarse == jnp.bfloat16(q), both, zero) for q in range(4)], 0)
-                )
-                within = jnp.broadcast_to(fine_bin[row : row + 1], (32, 128)).astype(jnp.bfloat16)
-                selectors[o].append(jnp.where(within == fine, jnp.bfloat16(1), jnp.bfloat16(0)))
-        for o in range(2):
-            total[o] += lax.dot_general(
-                jnp.concatenate(weights[o], 1),
-                jnp.concatenate(selectors[o], 1),
-                (((1,), (1,)), ((), ())),
-                preferred_element_type=jnp.float32,
-            )
-
-    @pl.when(step == pl.num_programs(0) - 1)
-    def _():
-        for o in range(2):
-            signal = jnp.zeros((1, NBIN), jnp.float32)
-            for q in range(8):
-                offset = q % 4 + q // 4
-                pieces = [
-                    total[o, 16 * g + q : 16 * g + q + 1, :] + total[o, 16 * g + 8 + q : 16 * g + 9 + q, :]
-                    for g in range(4)
-                ]
-                whole = jnp.concatenate(pieces, 1)
-                signal = signal + (pltpu.roll(whole, offset, 1) if offset else whole)
-            out_ref[o : o + 1, :] = signal
-
-
-def bin_call(lists, bins, fractions, gains, early, middle, late, state):
-    owned = pl.BlockSpec((NA, 1, PIECE, 128), lambda s: (0, s, 0, 0))
-
-    def part(rows):
-        return pl.BlockSpec((1, 2, NA // 2, rows, 128), lambda s: (s, 0, 0, 0, 0))
-
-    slab = pl.BlockSpec((NV, ROWS // NB, NR), lambda s: (0, s, 0))
-    return pl.pallas_call(
-        bin_kernel,
-        grid=(NB,),
-        in_specs=[
-            pl.BlockSpec((1, NA, 128), lambda s: (s, 0, 0)),
-            owned,
-            owned,
-            owned,
-            part(8),
-            part(4),
-            part(4),
-            slab,
-        ],
-        out_specs=(pl.BlockSpec((2, NBIN), lambda s: (0, 0)), slab),
-        out_shape=(
-            jax.ShapeDtypeStruct((2, NBIN), jnp.float32),
-            jax.ShapeDtypeStruct((NV, ROWS, NR), jnp.float32),
-        ),
-        scratch_shapes=[pltpu.VMEM((2, 64, 32), jnp.float32)],
-        compiler_params=pltpu.CompilerParams(vmem_limit_bytes=24 << 20),
-        name="binning",
-    )(lists, bins, fractions, gains, early, middle, late, state)
+    )(x, damping, jacobians, face_weight, phase_shift, lists, counts, bins, fractions, gains)
 
 
 def local(
@@ -754,7 +806,7 @@
 
     rest = elsewhere(zero) & elsewhere(last) & elsewhere(opposite)
     free = jnp.min(jnp.where(rest, jnp.arange(4, dtype=jnp.int32), 3))
-    state, lists, early, middle, late = lax.switch(
+    new_state, signal = lax.switch(
         free,
         [functools.partial(step_call, k) for k in range(4)],
         flow_state.reshape(NV, ROWS, NR),
@@ -764,16 +816,9 @@
         phase_shift,
         face_list[0].T,
         face_count,
-    )
-    signal, new_state = bin_call(
-        lists,
         arrival_bin.reshape(NA, NB, PIECE, 128),
         arrival_fraction.reshape(NA, NB, PIECE, 128),
         arrival_gain.reshape(NA, NB, PIECE, 128),
-        early,
-        middle,
-        late,
-        state,
     )
     return new_state.reshape(NV, CT, CZ, NR), signal
 

time: 57 us -> 54.8 us (0.961)
  Pallas kernels: 53.3 us -> 49.6 us
  local copies, waits for them, and re-layouts: 0.02 us -> 1.62 us
    pallas_call x1 -> x0, Pallas kernels: 9.22 us -> none  [bin_call(): pl.pallas_call(bin_kernel, grid=(NB,), in_specs=[pl.BlockSpec((1, NA, 128...]
    pallas_call x1, Pallas kernels: 44.1 us -> 49.6 us  [step_call(): pl.pallas_call(functools.partial(step_kernel, free), out_shape=(jax.Shape...]
    unnamed x6 -> x2, local copies, waits for them, and re-layouts: 0.02 us -> 1.62 us
where the time goes in v3:
time: 54.8 us; the launch traced here: 54.7 us
  Pallas kernels  49.6 us (91%)
  local copies, waits for them, and re-layouts  1.62 us (3%)
  other arithmetic  1.58 us (3%)
  between operations  1.29 us (2%)
  loops' own time  0.55 us (1%)
    pallas_call x1, Pallas kernels, step_call(): pl.pallas_call(functools.partial(step_kernel, free), out_shape=(jax.Shape...  49.6 us
    unnamed x2, local copies, waits for them, and re-layouts  1.62 us

profile of v3, /device:TPU:1, one launch (start us, length us, event | category | flops | bytes accessed | tf_op | source)
XLA Modules:
  0.0 54.7 jit_solution(315676319456447145)
XLA Ops:
  0.6 0.7 %broadcast_compare_fusion = (pred[4]{0:T(512)(128)(4,1)S(1)}, pred[4]{0:T(512)(128)(4,1)S(1)}, pred[4]{0:T(512)(128)(4,1)S(1)}) fusion(s32[4]{0:T(128)} %param.18), kind=kLoop, calls=%fused_computation.11 | loop fusion | flops 20 | bytes 28 | tf_op jit(solution)/shard_map/eq | solution.py:800
  1.3 0.1 fusion.4
  1.4 0.1 fusion.6
  1.6 0.6 %fusion.7 = s32[]{:T(128)} fusion(pred[4]{0:T(512)(128)(4,1)S(1)} %fusion.6, pred[4]{0:T(512)(128)(4,1)S(1)} %get-tuple-element.166, pred[4]{0:T(512)(128)(4,1)S(1)} %get-tuple-element.167), kind=kLoop, calls=%fused_computation.10 | loop fusion | flops 15 | bytes 16 | tf_op jit(solution)/shard_map/reduce_min | solution.py:808
  2.9 50.2 %conditional.1 = (f32[2,128]{1,0:T(2,128)S(1)}, f32[5,16,32,128]{3,2,1,0:T(8,128)S(1)}) conditional(s32[]{:T(128)} %clamp.3, (f32[5,16,32,128]{3,2,1,0:T(8,128)}, f32[16,32,128]{2,1,0:T(8,128)}, s32[1,128,4,2,128]{4,3,2,1,0:T(2,128)}, f32[1,128,4,2,128]{4,3,2,1,0:T(2,128)}, f32[1,128,4,2,128]{4,3,2,1,0:T(2,128)}, ...), branch_computations={%region_4.5_spmd, %region_5.6_spmd, %region_6.7_spmd, %region_7.8_... | conditional | bytes 16 | solution.py:809
  2.9 49.6 %substeps0.1 = (f32[5,512,128]{2,1,0:T(8,128)S(1)}, f32[2,128]{1,0:T(2,128)S(1)}) custom-call(f32[5,512,128]{2,1,0:T(8,128)} %bitcast.28, f32[512,128]{1,0:T(8,128)} %bitcast.44, f32[5,3,5]{2,1,0:T(4,128)} %get-tuple-element.111.jac_hbm, f32[5,16,32]{2,1,0:T(8,128)} %get-tuple-element.112.fw_hbm, s32[4]{0:T(128)} %get-tuple-element.113.shift_hbm, ...), custom_call_target="tpu_custom_call" | custom-call | tf_op jit(solution)/shard_map/cond/branch_0_fun/substeps0/pallas_call | solution.py:740
  53.1 1.1 %copy.22 = f32[5,16,32,128]{3,2,1,0:T(8,128)} copy(f32[5,16,32,128]{3,2,1,0:T(8,128)S(1)} %get-tuple-element.178) | data formatting | bytes 2621440
  54.1 0.6 %copy.23 = f32[2,128]{1,0:T(2,128)} copy(f32[2,128]{1,0:T(2,128)S(1)} %get-tuple-element.179) | data formatting | bytes 2048

commit v4 on v3

--- a/solution.py
+++ b/solution.py
@@ -50,6 +50,8 @@
     fraction_ref,
     gain_ref,
     selector_ref,
+    first_scale,
+    last_scale,
     wide_ref,
     total,
     last_total,
@@ -500,6 +502,12 @@
     place = lax.broadcasted_iota(jnp.int32, (8, 128), 0)
     which_sample = place % 4
 
+    first_sign = jnp.where(place < 4, -1.0, 1.0).astype(jnp.float32)
+    first_shift = jnp.where(place < 4, 1.0, 0.0).astype(jnp.float32)
+    last_sign = jnp.where(place % 2 == 0, -1.0, 1.0).astype(jnp.float32)
+    last_shift = jnp.where(place % 2 == 0, 1.0, 0.0).astype(jnp.float32)
+    group = (place // 2).astype(jnp.float32)
+
     def prepare(n):
         @pl.loop(0, NA)
         def _(m):
@@ -511,6 +519,15 @@
                     within = jnp.broadcast_to(fine_bin[row : row + 1], (32, 128)).astype(jnp.bfloat16)
                     columns.append(jnp.where(within == fine, jnp.bfloat16(1), jnp.bfloat16(0)))
                 selector_ref[n, m, o] = jnp.concatenate(columns, 1)
+            coarse_bin = (bin_ref[m, n] >> 5).astype(jnp.float32)
+            gains = gain_ref[m, n]
+            fractions = fraction_ref[m, n]
+            for row in range(PIECE):
+                gain = spread(gains[row : row + 1])
+                fraction = spread(fractions[row : row + 1])
+                first_scale[n, m, row] = gain * (fraction * first_sign + first_shift)
+                scale = gain * (fraction * last_sign + last_shift)
+                last_scale[n, m, row] = jnp.where(spread(coarse_bin[row : row + 1]) == group, scale, 0.0)
 
     def widen():
         spot = lax.broadcasted_iota(jnp.int32, (128, 5 * 128), 0)
@@ -542,14 +559,9 @@
         )
 
     def bin_first(n):
-        low = place < 4
-        sign = jnp.where(low, -1.0, 1.0).astype(jnp.float32)
-        shift = jnp.where(low, 1.0, 0.0).astype(jnp.float32)
         zero = jnp.zeros((16, 128), jnp.bfloat16)
         sums = [jnp.zeros((64, 32), jnp.float32)] * 2
         for m in range(NA):
-            gain = gain_ref[m, n]
-            fraction = fraction_ref[m, n]
             coarse_bin = (bin_ref[m, n] >> 5).astype(jnp.float32)
             early = early_ref[n, m % 2, m // 2]
             middle = middle_ref[n, m % 2, m // 2]
@@ -563,7 +575,7 @@
                 received = chosen(n, m, c, blocks)
                 for o in range(2):
                     row = slice(2 * c + o, 2 * c + o + 1)
-                    both = halves(received * (spread(gain[row]) * (spread(fraction[row]) * sign + shift)))
+                    both = halves(received * first_scale[n, m, 2 * c + o])
                     coarse = jnp.broadcast_to(coarse_bin[row], (16, 128)).astype(jnp.bfloat16)
                     weights[o].append(
                         jnp.concatenate([jnp.where(coarse == jnp.bfloat16(q), both, zero) for q in range(4)], 0)
@@ -574,25 +586,15 @@
             total[o] += sums[o]
 
     def bin_last(n):
-        part = place % 2
-        group = (place // 2).astype(jnp.float32)
-        sign = jnp.where(part == 0, -1.0, 1.0).astype(jnp.float32)
-        shift = jnp.where(part == 0, 1.0, 0.0).astype(jnp.float32)
         sums = [jnp.zeros((16, 32), jnp.float32)] * 2
         for m in range(NA):
-            gain = gain_ref[m, n]
-            fraction = fraction_ref[m, n]
-            coarse_bin = (bin_ref[m, n] >> 5).astype(jnp.float32)
             late = late_ref[n, m % 2, m // 2]
             blocks = [spread(late[block : block + 1]) for block in range(4)]
             weights = [[], []]
             for c in range(4):
                 received = chosen(n, m, c, blocks)
                 for o in range(2):
-                    row = slice(2 * c + o, 2 * c + o + 1)
-                    scale = spread(gain[row]) * (spread(fraction[row]) * sign + shift)
-                    scale = jnp.where(spread(coarse_bin[row]) == group, scale, 0.0)
-                    weights[o].append(halves(received * scale))
+                    weights[o].append(halves(received * last_scale[n, m, 2 * c + o]))
             for o in range(2):
                 sums[o] = sums[o] + against(weights[o], n, m, o)
         for o in range(2):
@@ -754,6 +756,8 @@
             pltpu.VMEM((NA, NB, PIECE, 128), jnp.float32),
             pltpu.VMEM((NA, NB, PIECE, 128), jnp.float32),
             pltpu.VMEM((NB, NA, 2, 32, 512), jnp.bfloat16),
+            pltpu.VMEM((NB, NA, PIECE, 8, 128), jnp.float32),
+            pltpu.VMEM((NB, NA, PIECE, 8, 128), jnp.float32),
             pltpu.VMEM((NB, NA, 5 * 128), jnp.float32),
             pltpu.VMEM((2, 64, 32), jnp.float32),
             pltpu.VMEM((2, 16, 32), jnp.float32),
@@ -784,6 +788,60 @@
     )(x, damping, jacobians, face_weight, phase_shift, lists, counts, bins, fractions, gains)
 
 
+def settle_kernel(state_ref, signal_ref, state_hbm, signal_hbm, sem):
+    copies = [pltpu.make_async_copy(signal_ref, signal_hbm, sem.at[NV])]
+    copies += [pltpu.make_async_copy(state_ref.at[v], state_hbm.at[v], sem.at[v]) for v in range(NV)]
+    for copy in copies:
+        copy.start()
+    for copy in copies:
+        copy.wait()
+
+
+def settle(state, signal):
+    vmem = pl.BlockSpec(memory_space=pltpu.VMEM)
+    hbm = pl.BlockSpec(memory_space=pltpu.HBM)
+    return pl.pallas_call(
+        settle_kernel,
+        out_shape=(
+            jax.ShapeDtypeStruct((NV, ROWS, NR), jnp.float32),
+            jax.ShapeDtypeStruct((2, NBIN), jnp.float32),
+        ),
+        in_specs=[vmem, vmem],
+        out_specs=(hbm, hbm),
+        scratch_shapes=[pltpu.SemaphoreType.DMA((NV + 1,))],
+        compiler_params=pltpu.CompilerParams(vmem_limit_bytes=4 << 20),
+        name="settle",
+    )(state, signal)
+
+
+def free_kernel(shift_hbm, out_ref, shift_ref, sem):
+    copy = pltpu.make_async_copy(shift_hbm, shift_ref, sem.at[0])
+    copy.start()
+    copy.wait()
+    flags = []
+    for k in range(4):
+        r = shift_ref[k]
+        flags.append((r == 0, r == CT * NA - 1, jnp.logical_and(r >= 128, r < 144)))
+
+    def settled(k):
+        others = [flags[n] for n in range(4) if n != k]
+        found = [others[0][f] | others[1][f] | others[2][f] for f in range(3)]
+        return found[0] & found[1] & found[2]
+
+    out_ref[0] = jnp.where(settled(0), 0, jnp.where(settled(1), 1, jnp.where(settled(2), 2, 3)))
+
+
+def free_substep(phase_shift):
+    return pl.pallas_call(
+        free_kernel,
+        out_shape=jax.ShapeDtypeStruct((1,), jnp.int32),
+        in_specs=[pl.BlockSpec(memory_space=pltpu.HBM)],
+        out_specs=pl.BlockSpec(memory_space=pltpu.SMEM),
+        scratch_shapes=[pltpu.SMEM((4,), jnp.int32), pltpu.SemaphoreType.DMA((1,))],
+        name="free_substep",
+    )(phase_shift)[0]
+
+
 def local(
     flow_state,
     damping,
@@ -796,16 +854,7 @@
     arrival_fraction,
     arrival_gain,
 ):
-    zero = phase_shift == 0
-    last = phase_shift == CT * NA - 1
-    opposite = jnp.logical_and(phase_shift >= 128, phase_shift < 144)
-    apart = jnp.logical_not(jnp.eye(4, dtype=bool))
-
-    def elsewhere(flags):
-        return jnp.any(jnp.logical_and(apart, flags[None, :]), axis=1)
-
-    rest = elsewhere(zero) & elsewhere(last) & elsewhere(opposite)
-    free = jnp.min(jnp.where(rest, jnp.arange(4, dtype=jnp.int32), 3))
+    free = free_substep(phase_shift)
     new_state, signal = lax.switch(
         free,
         [functools.partial(step_call, k) for k in range(4)],
@@ -820,6 +869,7 @@
         arrival_fraction.reshape(NA, NB, PIECE, 128),
         arrival_gain.reshape(NA, NB, PIECE, 128),
     )
+    new_state, signal = settle(new_state, signal)
     return new_state.reshape(NV, CT, CZ, NR), signal
 
 

time: 54.8 us -> 53.9 us (0.984)
  Pallas kernels: 49.6 us -> 51.5 us
  local copies, waits for them, and re-layouts: 1.62 us -> 0 us
  other arithmetic: 1.58 us -> 0 us
    pallas_call x0 -> x2, Pallas kernels: none -> 2.32 us  [the longest x1 1.22 us: free_substep(): pl.pallas_call(free_kernel, out_shape=jax.ShapeDtypeStruct((1,), jnp.int3...]
    unnamed x2 -> x0, local copies, waits for them, and re-layouts: 1.62 us -> none
    eq x1 -> x0, other arithmetic: 0.66 us -> none  [local(): last = phase_shift == CT * NA - 1]
    reduce_min x1 -> x0, other arithmetic: 0.65 us -> none  [local(): free = jnp.min(jnp.where(rest, jnp.arange(4, dtype=jnp.int32), 3))]
where the time goes in v4:
time: 53.9 us; the launch traced here: 53.6 us
  Pallas kernels  51.5 us (96%)
  between operations  1.51 us (3%)
  loops' own time  0.55 us (1%)
    pallas_call x1, Pallas kernels, step_call(): pl.pallas_call(functools.partial(step_kernel, free), out_shape=(jax.Shape...  49.2 us
    pallas_call x1, Pallas kernels, free_substep(): pl.pallas_call(free_kernel, out_shape=jax.ShapeDtypeStruct((1,), jnp.int3...  1.22 us
    pallas_call x1, Pallas kernels, settle(): pl.pallas_call(settle_kernel, out_shape=(jax.ShapeDtypeStruct((NV, ROWS,...  1.11 us

profile of v4, /device:TPU:1, one launch (start us, length us, event | category | flops | bytes accessed | tf_op | source)
XLA Modules:
  0.0 53.6 jit_solution(4737393882352659750)
XLA Ops:
  0.6 1.2 %free_substep.1 = s32[1]{0:T(128)} custom-call(s32[4]{0:T(128)} %shift_hbm.1), custom_call_target="tpu_custom_call" | custom-call | tf_op jit(solution)/shard_map/free_substep/pallas_call | solution.py:835
  2.5 49.7 %conditional.1 = ((f32[5,512,128]{2,1,0:T(8,128)S(1)}, f32[2,128]{1,0:T(2,128)S(1)})) conditional(s32[]{:T(128)} %bitcast, (f32[5,512,128]{2,1,0:T(8,128)}, f32[512,128]{1,0:T(8,128)}, f32[5,3,5]{2,1,0:T(4,128)}, f32[5,16,32]{2,1,0:T(8,128)}, s32[4]{0:T(128)}, /*index=5*/s32[4,128]{1,0:T(4,128)}, s32[1,128]{1,0:T(1,128)}, ...), branch_computations={%region_0.0_spmd, %region_1.0_spmd, %region_2.0_spmd, %region_3.0_... | conditional | bytes 8 | solution.py:858
  2.5 49.2 %substeps0.1 = (f32[5,512,128]{2,1,0:T(8,128)S(1)}, f32[2,128]{1,0:T(2,128)S(1)}) custom-call(f32[5,512,128]{2,1,0:T(8,128)} %get-tuple-element.80.x_hbm, f32[512,128]{1,0:T(8,128)} %get-tuple-element.81.damp_hbm, f32[5,3,5]{2,1,0:T(4,128)} %get-tuple-element.82.jac_hbm, f32[5,16,32]{2,1,0:T(8,128)} %get-tuple-element.83.fw_hbm, ...), custom_call_target="tpu_custom_call" | custom-call | tf_op jit(solution)/shard_map/cond/branch_0_fun/substeps0/pallas_call | solution.py:742
  52.2 1.1 %settle.1 = (f32[5,512,128]{2,1,0:T(8,128)}, f32[2,128]{1,0:T(2,128)}) custom-call(f32[5,512,128]{2,1,0:T(8,128)S(1)} %get-tuple-element.126.state_ref, f32[2,128]{1,0:T(2,128)S(1)} %get-tuple-element.127.signal_ref), custom_call_target="tpu_custom_call" | custom-call | tf_op jit(solution)/shard_map/settle/pallas_call | solution.py:803
